TPU v7x, 32 devices: a whole 2x2x4 slice. The times are simulated.
32 devices in a mesh: dp: 16 (over z, y, core), blk: 2 (over x).
Axes of the slice: x: 2, y: 2, z: 4, core: 2. Of those that a mesh axis runs over, the one named last changes fastest.
Arguments:
- inputs: bfloat16 [16, 2, 1024, 768], P('dp', 'blk'), may hold values from -6 to 6
- cotangent: bfloat16 [16, 2, 1024, 768], P('dp', 'blk'), may hold values from -6 to 6
- lengths: int32 [16], P('dp'), may hold values from 1025 to 2048, as said below
- groups: int32 [16], P('dp'), may hold values from 0 to 1, as said below
- flip: int32 [16], P('dp'), may hold values from 0 to 1
- w_qkv: bfloat16 [768, 2304], replicated, may hold values from -0.21875 to 0.21875
- b_query: float32 [768], replicated, may hold values from -1.5 to 1.5
- b_value: float32 [768], replicated, may hold values from -1.5 to 1.5
- w_out: bfloat16 [768, 768], replicated, may hold values from -0.875 to 0.875
- b_out: float32 [768], replicated, may hold values from -1.5 to 1.5
- gain_one: float32 [768], replicated, may hold values from 0.5 to 1.5
- shift_one: float32 [768], replicated, may hold values from -1.5 to 1.5
- gain_two: float32 [768], replicated, may hold values from 0.5 to 1.5
- shift_two: float32 [768], replicated, may hold values from -1.5 to 1.5
- w_fc: bfloat16 [768, 3072], replicated, may hold values from -0.21875 to 0.21875
- b_fc: float32 [3072], replicated, may hold values from -1.5 to 1.5
- w_proj: bfloat16 [3072, 768], replicated, may hold values from -0.109375 to 0.109375
- b_proj: float32 [768], replicated, may hold values from -1.5 to 1.5
Outputs:
- block_out: bfloat16 [16, 2, 1024, 768], P('dp', 'blk')
- input_grad: bfloat16 [16, 2, 1024, 768], P('dp', 'blk')
- grad_w_qkv: float32 [768, 2304], replicated
- grad_b_query: float32 [768], replicated
- grad_b_value: float32 [768], replicated
- grad_w_out: float32 [768, 768], replicated
- grad_b_out: float32 [768], replicated
- grad_gain_one: float32 [768], replicated
- grad_shift_one: float32 [768], replicated
- grad_gain_two: float32 [768], replicated
- grad_shift_two: float32 [768], replicated
- grad_w_fc: float32 [768, 3072], replicated
- grad_b_fc: float32 [3072], replicated
- grad_w_proj: float32 [3072, 768], replicated
- grad_b_proj: float32 [768], replicated
- group_rms: float32 [2, 3], replicated
Inputs may be any that keep to these rules, and one draw needn't show every extreme that they name: Both groups are present; group 0 lengths exceed 3 * 512 and some reaches 2048; group 1 lengths exceed 1024 and some equals 1536. Each of the two groups holds at least one sequence.
All inputs are finite; a program needn't handle non-finite values.
Results may differ from a plain program's by a relative error of at most 0.012.
Values may be sent and summed in bfloat16 or wider, within the bound.
No kernel may reach another device: no remote copies, remote signals or barrier semaphores. Data moves between devices by JAX's collectives and lax.ppermute only.
A program may use at most 320 MiB of HBM per device.

v0:
```python
import jax
import jax.numpy as jnp
from jax import lax
from jax.sharding import PartitionSpec as P

HD = 64


EPS = 1e-05


def from_partner(array, axis, bit):
    return lax.ppermute(array, axis, [(i, i ^ 1 << bit) for i in range(lax.axis_size(axis))])


def normalize(values, gain, shift):
    centered = values - jnp.mean(values, -1, keepdims=True)
    inv_std = lax.rsqrt(jnp.mean(centered * centered, -1, keepdims=True) + EPS)
    x_hat = centered * inv_std
    return (x_hat * gain + shift, x_hat, inv_std)


def norm_back(upstream, x_hat, inv_std, gain):
    scaled = upstream * gain
    inner = (
        scaled
        - jnp.mean(scaled, -1, keepdims=True)
        - x_hat * jnp.mean(scaled * x_hat, -1, keepdims=True)
    )
    return (inv_std * inner, jnp.sum(upstream * x_hat, 0), jnp.sum(upstream, 0))


def contract_rows(left, right):
    return lax.dot_general(
        left, right, (((0,), (0,)), ((), ())), preferred_element_type=jnp.float32
    )


def times_trans(left, right):
    return lax.dot_general(
        left, right, (((1,), (1,)), ((), ())), preferred_element_type=jnp.float32
    )


def body(
    inputs,
    cotangent,
    lengths,
    groups,
    flip,
    w_qkv,
    b_query,
    b_value,
    w_out,
    b_out,
    gain_one,
    shift_one,
    gain_two,
    shift_two,
    w_fc,
    b_fc,
    w_proj,
    b_proj,
):
    span_len = inputs.shape[2]
    width = inputs.shape[3]
    n_heads = width // HD
    scale = HD ** (-0.5)
    my_place = jnp.bitwise_xor(lax.axis_index("blk"), flip[0])
    other_place = 1 - my_place
    length = lengths[0]
    row_ids = jnp.arange(span_len, dtype=jnp.int32)
    local_pos = my_place * span_len + row_ids
    remote_pos = other_place * span_len + row_ids
    x_in = inputs[0, 0].astype(jnp.float32)
    normed_f, x_hat_one, inv_one = normalize(x_in, gain_one, shift_one)
    normed = normed_f.astype(jnp.bfloat16)
    qkv = jnp.dot(normed, w_qkv, preferred_element_type=jnp.float32)
    query = (qkv[:, :width] + b_query).astype(jnp.bfloat16)
    kv_bias = jnp.concatenate([jnp.zeros_like(b_value), b_value])
    key_value = (qkv[:, width:] + kv_bias).astype(jnp.bfloat16)
    remote_kv = from_partner(key_value, "blk", 0)
    local_keys = key_value[:, :width].reshape(span_len, n_heads, HD)
    local_values = key_value[:, width:].reshape(span_len, n_heads, HD)
    remote_keys = remote_kv[:, :width].reshape(span_len, n_heads, HD)
    remote_values = remote_kv[:, width:].reshape(span_len, n_heads, HD)
    block_rows = min(512, span_len)
    n_blocks = span_len // block_rows

    def visible_keys(q_index, with_remote):
        stop = (q_index + 1) * block_rows
        keys = local_keys[:stop]
        values = local_values[:stop]
        places = local_pos[:stop]
        if with_remote:
            keys = jnp.concatenate([remote_keys, keys], 0)
            values = jnp.concatenate([remote_values, values], 0)
            places = jnp.concatenate([remote_pos, places], 0)
        return (keys, values, places)

    def block_scores(q_index, keys, places):
        offset = q_index * block_rows
        q_block = query[offset : offset + block_rows].reshape(block_rows, n_heads, HD)
        scores = (
            jnp.einsum("qhd,khd->hqk", q_block, keys, preferred_element_type=jnp.float32) * scale
        )
        q_pos = my_place * span_len + offset + jnp.arange(block_rows, dtype=jnp.int32)
        allowed = (places[None, :] <= q_pos[:, None]) & (places[None, :] < length)
        return (q_block, jnp.where(allowed[None], scores, -1e30))

    def forward_pass(with_remote):
        att_parts = []
        sum_parts = []
        for q_index in range(n_blocks):
            keys, values, places = visible_keys(q_index, with_remote)
            q_block, scores = block_scores(q_index, keys, places)
            row_max = jnp.max(scores, -1, keepdims=True)
            expo = jnp.exp(scores - row_max)
            row_sum = jnp.sum(expo, -1, keepdims=True)
            probs = (expo / row_sum).astype(jnp.bfloat16)
            attended_block = jnp.einsum(
                "hqk,khd->qhd", probs, values, preferred_element_type=jnp.float32
            )
            att_parts.append(attended_block.reshape(block_rows, width).astype(jnp.bfloat16))
            sum_parts.append(row_max + jnp.log(row_sum))
        return (jnp.concatenate(att_parts, 0), jnp.stack(sum_parts, 0))

    attended, log_sums = lax.cond(
        my_place == 1, lambda: forward_pass(True), lambda: forward_pass(False)
    )
    branch_att = jnp.dot(attended, w_out, preferred_element_type=jnp.float32) + b_out
    middle = x_in + branch_att
    normed_two_f, x_hat_two, inv_two = normalize(middle, gain_two, shift_two)
    normed_two = normed_two_f.astype(jnp.bfloat16)
    pre_act = jnp.dot(normed_two, w_fc, preferred_element_type=jnp.float32) + b_fc
    gelu_val, gelu_back = jax.vjp(lambda val: jax.nn.gelu(val, approximate=True), pre_act)
    activ = gelu_val.astype(jnp.bfloat16)
    branch_mlp = jnp.dot(activ, w_proj, preferred_element_type=jnp.float32) + b_proj
    outputs = middle + branch_mlp
    upstream_b = cotangent[0, 0]
    upstream = upstream_b.astype(jnp.float32)
    grad_w_proj = contract_rows(activ, upstream_b)
    grad_b_proj = jnp.sum(upstream, 0)
    grad_pre = gelu_back(times_trans(upstream_b, w_proj))[0].astype(jnp.bfloat16)
    grad_w_fc = contract_rows(normed_two, grad_pre)
    grad_b_fc = jnp.sum(grad_pre.astype(jnp.float32), 0)
    grad_normed_two = times_trans(grad_pre, w_fc)
    grad_mid_norm, grad_gain_two, grad_shift_two = norm_back(
        grad_normed_two, x_hat_two, inv_two, gain_two
    )
    grad_middle = upstream + grad_mid_norm
    grad_att = grad_middle.astype(jnp.bfloat16)
    grad_w_out = contract_rows(attended, grad_att)
    grad_b_out = jnp.sum(grad_att.astype(jnp.float32), 0)
    grad_attended = times_trans(grad_att, w_out).astype(jnp.bfloat16)

    def backward_pass(with_remote):
        local_total = jnp.zeros((span_len, 2 * width), jnp.float32)
        remote_total = jnp.zeros((span_len, 2 * width), jnp.float32)
        q_parts = []
        for q_index in range(n_blocks):
            offset = q_index * block_rows
            stop = offset + block_rows
            keys, values, places = visible_keys(q_index, with_remote)
            q_block, scores = block_scores(q_index, keys, places)
            probs = jnp.exp(scores - log_sums[q_index])
            grad_block = grad_attended[offset:stop].reshape(block_rows, n_heads, HD)
            grad_probs = jnp.einsum(
                "qhd,khd->hqk", grad_block, values, preferred_element_type=jnp.float32
            )
            grad_scores = (
                probs * (grad_probs - jnp.sum(probs * grad_probs, -1, keepdims=True))
            ).astype(jnp.bfloat16)
            grad_q = (
                jnp.einsum("hqk,khd->qhd", grad_scores, keys, preferred_element_type=jnp.float32)
                * scale
            )
            grad_k = (
                jnp.einsum("hqk,qhd->khd", grad_scores, q_block, preferred_element_type=jnp.float32)
                * scale
            )
            grad_v = jnp.einsum(
                "hqk,qhd->khd",
                probs.astype(jnp.bfloat16),
                grad_block,
                preferred_element_type=jnp.float32,
            )
            n_keys = keys.shape[0]
            grad_kv = jnp.concatenate(
                [grad_k.reshape(n_keys, width), grad_v.reshape(n_keys, width)], 1
            )
            if with_remote:
                remote_total = remote_total + grad_kv[:span_len]
                grad_kv = grad_kv[span_len:]
            local_total = local_total + jnp.pad(grad_kv, ((0, span_len - stop), (0, 0)))
            q_parts.append(grad_q.reshape(block_rows, width))
        return (local_total, remote_total, jnp.concatenate(q_parts, 0))

    local_total, remote_total, grad_q_all = lax.cond(
        my_place == 1, lambda: backward_pass(True), lambda: backward_pass(False)
    )
    returned = from_partner(remote_total, "blk", 0)
    grad_kv_local = (local_total + returned).astype(jnp.bfloat16)
    grad_query = grad_q_all.astype(jnp.bfloat16)
    grad_qkv = jnp.concatenate([grad_query, grad_kv_local], 1)
    grad_b_query = jnp.sum(grad_query.astype(jnp.float32), 0)
    grad_b_value = jnp.sum(grad_kv_local[:, width:].astype(jnp.float32), 0)
    grad_w_qkv = contract_rows(normed, grad_qkv)
    grad_normed = times_trans(grad_qkv, w_qkv)
    grad_x_norm, grad_gain_one, grad_shift_one = norm_back(
        grad_normed, x_hat_one, inv_one, gain_one
    )
    input_grad = (grad_middle + grad_x_norm).astype(jnp.bfloat16)
    valid = (local_pos < length).astype(jnp.float32)
    member = (groups[0] == jnp.arange(2, dtype=jnp.int32)).astype(jnp.float32)
    squares = jnp.stack(
        [
            jnp.sum(outputs * outputs, -1),
            jnp.sum(branch_att * branch_att, -1),
            jnp.sum(branch_mlp * branch_mlp, -1),
        ],
        0,
    )
    local_sums = member[:, None] * jnp.sum(squares * valid[None, :], 1)[None, :]
    local_counts = member * jnp.sum(valid)
    summed = lax.psum(
        (
            grad_w_qkv,
            grad_b_query,
            grad_b_value,
            grad_w_out,
            grad_b_out,
            grad_gain_one,
            grad_shift_one,
            grad_gain_two,
            grad_shift_two,
            grad_w_fc,
            grad_b_fc,
            grad_w_proj,
            grad_b_proj,
            local_sums,
            local_counts,
        ),
        ("dp", "blk"),
    )
    group_sums = summed[13]
    counts = summed[14]
    group_rms = jnp.sqrt(group_sums / (counts[:, None] * width))
    return (
        outputs.astype(jnp.bfloat16)[None, None],
        input_grad[None, None],
        summed[0],
        summed[1],
        summed[2],
        summed[3],
        summed[4],
        summed[5],
        summed[6],
        summed[7],
        summed[8],
        summed[9],
        summed[10],
        summed[11],
        summed[12],
        group_rms,
    )


def solution(mesh):
    placed = (
        P("dp", "blk", None, None),
        P("dp", "blk", None, None),
        P("dp"),
        P("dp"),
        P("dp"),
        P(),
        P(),
        P(),
        P(),
        P(),
        P(),
        P(),
        P(),
        P(),
        P(),
        P(),
        P(),
        P(),
    )
    return jax.shard_map(
        body,
        mesh=mesh,
        in_specs=placed,
        out_specs=(
            P("dp", "blk", None, None),
            P("dp", "blk", None, None),
            P(),
            P(),
            P(),
            P(),
            P(),
            P(),
            P(),
            P(),
            P(),
            P(),
            P(),
            P(),
            P(),
            P(),
        ),
        check_vma=False,
    )
```

profile of v0, /device:TPU:0, one launch (start us, length us, event | category | flops | bytes accessed | tf_op | source)
XLA Modules:
  0.0 1233.0 jit_solution(17526577108923374738)
XLA Ops:
  14.2 5.7 fusion.147
  42.9 53.0 %collective-permute-done = bf16[1024,1536]{1,0:T(8,128)(2,1)} collective-permute-done((bf16[1024,1536]{1,0:T(8,128)(2,1)}, bf16[1024,1536]{1,0:T(8,128)(2,1)}, u32[]{:S(2)}, u32[]{:S(2)}) %collective-permute-start) | collective-permute-done | bytes 3145760 | tf_op jit(solution)/shard_map/ppermute | solution.py:13
  104.9 74.7 %conditional.4 = (bf16[1024,768]{0,1:T(8,128)(2,1)S(1)}, f32[2,12,512,1]{2,1,3,0:T(8,128)S(1)}) conditional(s32[]{:T(128)} %convert_element_type.158, (s32[1024]{0:T(1024)S(1)}, s32[]{:T(128)}, s32[]{:T(128)}, bf16[1024,768]{1,0:T(8,128)(2,1)}, bf16[1024,12,64]{0,2,1:T(8,128)(2,1)}, /*index=5*/bf16[1024,12,64]{0,2,1:T(8,128)(2,1)}) %tuple.110, ...), branch_computations={%region_2.7_spmd, %region_7.12_spmd} | conditional | flops 5931015680 | bytes 331590976 | solution.py:128
  111.9 12.2 fusion
  124.1 12.3 fusion.1
  139.5 9.5 fusion.7
  150.0 6.9 fusion.3
  156.9 7.9 fusion.4
  185.5 12.9 %multiply_convert_fusion.2 = (bf16[1024,3072]{1,0:T(8,128)(2,1)}, f32[1024,3072]{1,0:T(8,128)}) fusion(f32[3072]{0:T(1024)S(1)} %copy-done.81, bf16[768,3072]{1,0:T(8,128)(2,1)S(1)} %copy-done.79, f32[1024,768]{0,1:T(8,128)S(1)} %get-tuple-element.322, f32[768]{0:T(1024)S(1)} %copy-done.83, f32[768]{0:T(1024)S(1)} %copy-done.74, ...), kind=kOutput, calls=%fused_computation.195 | convolution fusion | flops 4867227648 | bytes 26765312 | tf_op jit(solution)/shard_map/dot_general | solution.py:135
  198.5 16.8 %convert_reduce_fusion = (f32[3072]{0:T(1024)}, bf16[1024,3072]{1,0:T(8,128)(2,1)}) fusion(f32[1024,3072]{1,0:T(8,128)} %get-tuple-element.369, f32[3072]{0:T(1024)S(1)} %copy-done.81, bf16[3072,768]{1,0:T(8,128)(2,1)S(1)} %bitcast.319, bf16[1,1,1024,768]{3,2,1,0:T(8,128)(2,1)S(1)} %copy-done.49), kind=kOutput, calls=%fused_computation.194 | convolution fusion | flops 4904186880 | bytes 25190400 | tf_op jit(solution)/shard_map/dot_general | solution.py:40
  215.3 9.1 fusion.162
  227.9 13.1 %multiply_reduce_fusion.4 = (f32[1024]{0:T(1024)}, f32[1024]{0:T(1024)}, f32[1024]{0:T(1024)S(1)}, f32[1024]{0:T(1024)S(1)}, f32[768]{0:T(1024)}, /*index=5*/bf16[1,1,1024,768]{2,3,1,0:T(8,128)(2,1)}) fusion(f32[1024,768]{0,1:T(8,128)} %copy-done.25, f32[768]{0:T(1024)} %param.39, f32[1024,768]{0,1:T(8,128)} %copy.122, f32[768]{0:T(1024)} %param.34, ...), kind=kOutput, calls=%fused_computation.225 | convolution fusion | flops 4843629568 | bytes 18908160 | tf_op jit(solution)/shard_map/dot_general | solution.py:138
  247.6 158.4 %conditional.12 = (f32[1024,1536]{0,1:T(8,128)}, f32[1024,1536]{0,1:T(8,128)}, bf16[1024,768]{0,1:T(8,128)(2,1)S(1)}) conditional(s32[]{:T(128)} %convert_element_type.158, (s32[1024]{0:T(1024)S(1)}, s32[]{:T(128)}, s32[]{:T(128)}, bf16[1024,768]{1,0:T(8,128)(2,1)}, bf16[1024,12,64]{0,2,1:T(8,128)(2,1)}, /*index=5*/f32[2,12,512,1]{2,1,3,0:T(8,128)}, ...), branch_computations={%region_16.19_spmd, %region_19.22_spmd} | conditional | flops 14468902912 | bytes 835349696
  258.2 7.8 fusion.61
  267.5 9.1 fusion.55
  276.7 11.3 multiply_reduce_fusion.1
  289.3 7.0 multiply_convert_fusion.1
  299.7 10.1 fusion.163
  310.9 13.6 %fusion.50 = f32[12,1024,64]{1,2,0:T(8,128)} fusion(bf16[512,12,64]{0,2,1:T(8,128)(2,1)} %bitcast.304, f32[12,512,1024]{2,1,0:T(8,128)} %fusion.163, f32[12,512]{1,0:T(8,128)} %get-tuple-element.343, pred[512,1024]{1,0:T(8,128)(4,1)S(1)} %compare_and_fusion.4), kind=kOutput, calls=%fused_computation.87 | convolution fusion | flops 830472192 | bytes 29646848 | tf_op jit(solution)/shard_map/cond/branch_0_fun/hqk,qhd->khd/dot_general | solution.py:182
  324.5 18.8 %multiply_reduce_fusion = (f32[12,512]{1,0:T(8,128)}, f32[12,512,1024]{2,1,0:T(8,128)}) fusion(f32[12,512,1024]{2,1,0:T(8,128)} %fusion.163, f32[12,512]{1,0:T(8,128)} %get-tuple-element.343, pred[512,1024]{1,0:T(8,128)(4,1)} %copy-done.41, bf16[512,12,64]{0,2,1:T(8,128)(2,1)} %bitcast.305, bf16[1024,12,64]{0,2,1:T(8,128)(2,1)} %get-tuple-element.100), kind=kOutput, calls=%fused_computation.81 | convolution fusion | flops 836757504 | bytes 53264384 | tf_op jit(solution)/shard_map/cond/branch_0_fun/qhd,khd->hqk/dot_general | solution.py:168
  343.3 17.3 %multiply_convert_fusion = bf16[12,512,1024]{2,1,0:T(8,128)(2,1)S(1)} fusion(f32[12,512,1024]{2,1,0:T(8,128)} %get-tuple-element.348, f32[12,512,1024]{2,1,0:T(8,128)} %fusion.163, f32[12,512]{1,0:T(8,128)} %get-tuple-element.347, f32[12,512]{1,0:T(8,128)} %get-tuple-element.343, pred[512,1024]{1,0:T(8,128)(4,1)} %copy-done.41), kind=kLoop, calls=%fused_computation.80 | loop fusion | flops 37748736 | bytes 63488000 | tf_op jit(solution)/shard_map/cond/branch_0_fun/convert_element_type | solution.py:173
  373.8 9.8 convolution_multiply_fusion.3
  407.2 215.7 %collective-permute-start.1 = (f32[1024,1536]{0,1:T(8,128)}, f32[1024,1536]{0,1:T(8,128)S(1)}, u32[]{:S(2)}, u32[]{:S(2)}) collective-permute-start(f32[1024,1536]{0,1:T(8,128)} %get-tuple-element.137), channel_id=1, source_target_pairs={{0,1},{1,0},{2,3},{3,2},{4,5},{5,4},{6,7},{7,6},{8,9},{9,8},{10,11... | collective-permute-start | bytes 18874376 | tf_op jit(solution)/shard_map/ppermute | solution.py:13
  628.3 7.8 fusion.149
  636.2 7.8 fusion.136
  644.0 114.1 %collective-permute-done.1 = f32[1024,1536]{0,1:T(8,128)S(1)} collective-permute-done((f32[1024,1536]{0,1:T(8,128)}, f32[1024,1536]{0,1:T(8,128)S(1)}, u32[]{:S(2)}, u32[]{:S(2)}) %collective-permute-start.1) | collective-permute-done | bytes 6291488 | tf_op jit(solution)/shard_map/ppermute | solution.py:13
  763.8 7.1 fusion.133
  781.3 8.6 fusion.161
  806.9 42.6 %all-reduce.3 = (f32[768]{0:T(1024)}, f32[768]{0:T(1024)}, f32[768]{0:T(1024)}, f32[768]{0:T(1024)}, f32[768]{0:T(1024)}, /*index=5*/f32[768]{0:T(1024)}, f32[76...) all-reduce(f32[768]{0:T(1024)S(1)} %convert_reduce_fusion.5, ...), channel_id=1, replica_groups=mesh['dp'=16,'blk'=2] {'dp','blk'}, use_global_device_ids=true, to_apply=%region_26.27 | all-reduce | flops 9224 | bytes 73792 | tf_op jit(solution)/shard_map/psum | solution.py:226
  851.4 353.2 %all-reduce.7.cloned.1.call-done = (f32[768,2304]{1,0:T(8,128)}, f32[768,768]{1,0:T(8,128)}, f32[768,3072]{1,0:T(8,128)}, f32[3072,768]{1,0:T(8,128)}) async-done(((f32[768,2304]{1,0:T(8,128)}, f32[768,768]{1,0:T(8,128)}, f32[768,3072]{1,0:T(8,128)}, f32[3072,768]{1,0:T(8,128)}), (f32[768,2304]{1,0:T(8,128)}, f32[768,768]{1,0:T(8,128)}, f32[768,3072]{1,0:T(8,128)}, ...) | async-done | bytes 28311568 | tf_op jit(solution)/shard_map/psum | solution.py:226
  1204.7 6.6 copy.164
  1212.6 9.3 copy.166
  (244 shorter events, 154.6 us)
Async XLA Ops:
  7.2 1197.4 %all-reduce.7.cloned.1.call-start = ((), (), s32[]{:S(2)}) async-start(), calls=%async_computation | async-start | bytes 56623104 | tf_op jit(solution)/shard_map/psum | solution.py:226
  24.6 71.4 %collective-permute-start = (bf16[1024,1536]{1,0:T(8,128)(2,1)}, bf16[1024,1536]{1,0:T(8,128)(2,1)}, u32[]{:S(2)}, u32[]{:S(2)}) collective-permute-start(bf16[1024,1536]{1,0:T(8,128)(2,1)} %fusion.114), channel_id=1, source_target_pairs={{0,1},{1,0},{2,3},{3,2},{4,5},{5,4},{6,7},{7,6},{8,9},{9,8},{10,11... | collective-permute-start | bytes 9437192 | tf_op jit(solution)/shard_map/ppermute | solution.py:13
  104.9 75.3 %copy-start.82 = (f32[768]{0:T(1024)S(1)}, f32[768]{0:T(1024)}, u32[]{:S(2)}) copy-start(f32[768]{0:T(1024)} %param.31) | copy-start | bytes 9220
  111.9 12.2 copy-start.42
  111.9 24.5 %copy-start.11 = (bf16[1024,12,64]{0,2,1:T(8,128)(2,1)S(1)}, bf16[1024,12,64]{0,2,1:T(8,128)(2,1)}, u32[]{:S(2)}) copy-start(bf16[1024,12,64]{0,2,1:T(8,128)(2,1)} %get-tuple-element.83) | copy-start | bytes 4718596 | tf_op jit(solution)/shard_map/cond
  124.1 15.4 %copy-start.1 = (f32[12,512,1024]{2,1,0:T(8,128)S(1)}, f32[12,512,1024]{2,1,0:T(8,128)}, u32[]{:S(2)}) copy-start(f32[12,512,1024]{2,1,0:T(8,128)} %get-tuple-element.326) | copy-start | bytes 75497472 | tf_op jit(solution)/shard_map/cond
  139.5 10.5 copy-start.2
  185.0 13.4 %copy-start.25 = (f32[1024,768]{0,1:T(8,128)}, f32[1024,768]{0,1:T(8,128)S(1)}, u32[]{:S(2)}) copy-start(f32[1024,768]{0,1:T(8,128)S(1)} %get-tuple-element.322) | copy-start | bytes 9437188
  185.0 55.9 %copy-start.65 = (f32[1024]{0:T(1024)}, f32[1024]{0:T(1024)S(1)}, u32[]{:S(2)}) copy-start(f32[1024]{0:T(1024)S(1)} %broadcast_multiply_fusion.4) | copy-start | bytes 12292
  185.0 13.4 %slice-start.6 = ((s8[4718592]{0:T(1024)(128)(4,1)}), s8[4194304]{0:T(1024)(128)(4,1)S(1)}, s32[]{:S(2)}) async-start(s8[4718592]{0:T(1024)(128)(4,1)} %bitcast.318), calls=%async_computation.7 | async-start | bytes 8388608
  185.5 55.5 %copy-start.72 = (f32[1024]{0:T(1024)}, f32[1024]{0:T(1024)S(1)}, u32[]{:S(2)}) copy-start(f32[1024]{0:T(1024)S(1)} %add_rsqrt_fusion) | copy-start | bytes 12292
  185.5 12.9 %copy-start.49 = (bf16[1,1,1024,768]{3,2,1,0:T(8,128)(2,1)S(1)}, bf16[1,1,1024,768]{3,2,1,0:T(8,128)(2,1)}, u32[]{:S(2)}) copy-start(bf16[1,1,1024,768]{3,2,1,0:T(8,128)(2,1)} %param.23) | copy-start | bytes 4718596
  185.5 12.9 %slice-start.7 = ((s8[4718592]{0:T(1024)(128)(4,1)}), s8[524288]{0:T(1024)(128)(4,1)S(1)}, s32[]{:S(2)}) async-start(s8[4718592]{0:T(1024)(128)(4,1)} %bitcast.318), calls=%async_computation.8 | async-start | bytes 1048576
  227.9 13.1 %copy-start.26 = (f32[1024,768]{0,1:T(8,128)S(1)}, f32[1024,768]{0,1:T(8,128)}, u32[]{:S(2)}) copy-start(f32[1024,768]{0,1:T(8,128)} %copy-done.25) | copy-start | bytes 9437188
  227.9 13.1 %copy-start.28 = (f32[1024,768]{0,1:T(8,128)S(1)}, f32[1024,768]{0,1:T(8,128)}, u32[]{:S(2)}) copy-start(f32[1024,768]{0,1:T(8,128)} %copy.122) | copy-start | bytes 9437188
  227.9 13.1 %copy-start.38 = (bf16[1,1,1024,768]{2,3,1,0:T(8,128)(2,1)S(1)}, bf16[1,1,1024,768]{2,3,1,0:T(8,128)(2,1)}, u32[]{:S(2)}) copy-start(bf16[1,1,1024,768]{2,3,1,0:T(8,128)(2,1)} %copy.121) | copy-start | bytes 4718596
  227.9 13.1 %copy-start.75 = (f32[768]{0:T(1024)S(1)}, f32[768]{0:T(1024)}, u32[]{:S(2)}) copy-start(f32[768]{0:T(1024)} %param.34) | copy-start | bytes 9220
  276.7 11.3 slice-start
  276.7 11.3 slice-start.1
  276.7 12.6 %slice-start.2 = ((s8[12582912]{0:T(1024)(128)(4,1)}), s8[4194304]{0:T(1024)(128)(4,1)S(1)}, s32[]{:S(2)}) async-start(s8[12582912]{0:T(1024)(128)(4,1)} %bitcast.263), calls=%async_computation.3 | async-start | bytes 8388608
  296.4 13.5 %copy-start.6 = (bf16[12,512,512]{1,2,0:T(8,128)(2,1)}, bf16[12,512,512]{1,2,0:T(8,128)(2,1)S(1)}, u32[]{:S(2)}) copy-start(bf16[12,512,512]{1,2,0:T(8,128)(2,1)S(1)} %multiply_convert_fusion.1) | copy-start | bytes 18874372
  310.9 13.6 %copy-start.41 = (pred[512,1024]{1,0:T(8,128)(4,1)}, pred[512,1024]{1,0:T(8,128)(4,1)S(1)}, u32[]{:S(2)}) copy-start(pred[512,1024]{1,0:T(8,128)(4,1)S(1)} %compare_and_fusion.4) | copy-start | bytes 1572868
  343.3 17.4 %copy-start.23 = (bf16[512,768]{0,1:T(8,128)(2,1)S(1)}, bf16[512,768]{0,1:T(8,128)(2,1)}, u32[]{:S(2)}) copy-start(bf16[512,768]{0,1:T(8,128)(2,1)} %get-tuple-element.339) | copy-start | bytes 2359300
  407.2 221.1 %copy-start.27 = (f32[1024,768]{0,1:T(8,128)S(1)}, f32[1024,768]{0,1:T(8,128)}, u32[]{:S(2)}) copy-start(f32[1024,768]{0,1:T(8,128)} %copy-done.25) | copy-start | bytes 9437188
  407.2 221.1 %copy-start.66 = (f32[1024]{0:T(1024)S(1)}, f32[1024]{0:T(1024)}, u32[]{:S(2)}) copy-start(f32[1024]{0:T(1024)} %copy-done.65) | copy-start | bytes 12292
  407.2 221.1 %copy-start.73 = (f32[1024]{0:T(1024)S(1)}, f32[1024]{0:T(1024)}, u32[]{:S(2)}) copy-start(f32[1024]{0:T(1024)} %copy-done.72) | copy-start | bytes 12292
  407.2 221.1 %copy-start.76 = (f32[768]{0:T(1024)S(1)}, f32[768]{0:T(1024)}, u32[]{:S(2)}) copy-start(f32[768]{0:T(1024)} %param.34) | copy-start | bytes 9220
  407.2 221.1 %copy-start.84 = (f32[768]{0:T(1024)S(1)}, f32[768]{0:T(1024)}, u32[]{:S(2)}) copy-start(f32[768]{0:T(1024)} %param.35) | copy-start | bytes 9220
  407.2 221.1 %copy-start.87 = (bf16[1024,3072]{1,0:T(8,128)(2,1)S(1)}, bf16[1024,3072]{1,0:T(8,128)(2,1)}, u32[]{:S(2)}) copy-start(bf16[1024,3072]{1,0:T(8,128)(2,1)} %get-tuple-element.375) | copy-start | bytes 18874372
  407.2 350.8 %collective-permute-start.1 = (f32[1024,1536]{0,1:T(8,128)}, f32[1024,1536]{0,1:T(8,128)S(1)}, u32[]{:S(2)}, u32[]{:S(2)}) collective-permute-start(f32[1024,1536]{0,1:T(8,128)} %get-tuple-element.137), channel_id=1, source_target_pairs={{0,1},{1,0},{2,3},{3,2},{4,5},{5,4},{6,7},{7,6},{8,9},{9,8},{10,11... | collective-permute-start | bytes 18874376 | tf_op jit(solution)/shard_map/ppermute | solution.py:13
  622.9 13.2 %slice-start.8 = ((s8[6291456]{0:T(1024)(128)(4,1)}), s8[4194304]{0:T(1024)(128)(4,1)S(1)}, s32[]{:S(2)}) async-start(s8[6291456]{0:T(1024)(128)(4,1)} %bitcast.320), calls=%async_computation.9 | async-start | bytes 8388608
  1211.2 10.7 slice-start.3
  (51 other events, 288.0 us)
Sparse Core Ops, SparseCore 0:
  771.1 433.5 all-reduce.6
where the time goes:
time: 1240 us; the launch traced here: 1230 us
  waiting for transfers between devices  520 us (42%)
  matrix products  225 us (18%)
  starting transfers between devices  219 us (18%)
  local copies, waits for them, and re-layouts  94.3 us (8%)
  other arithmetic  90.5 us (7%)
  blocking collectives  42.6 us (3%)
  loops' own time  24.4 us (2%)
  between operations  16.9 us (1%)
    psum x1, waiting for transfers between devices, body(): lax.psum((grad_w_qkv, grad_b_query, grad_b_value, grad_w_out, grad_b_out,...  353 us
    ppermute x2, starting transfers between devices, from_partner(): lax.ppermute(array, axis, [(i, i ^ 1 << bit) for i in range(lax.axis_size...  219 us
    ppermute x2, waiting for transfers between devices, from_partner(): lax.ppermute(array, axis, [(i, i ^ 1 << bit) for i in range(lax.axis_size...  167 us
    unnamed x152, local copies, waits for them, and re-layouts  46.3 us
    psum x1, blocking collectives, body(): lax.psum((grad_w_qkv, grad_b_query, grad_b_value, grad_w_out, grad_b_out,...  42.6 us
    dot_general x4, matrix products, times_trans(): lax.dot_general(left, right, (((1,), (1,)), ((), ())), preferred_element_...  37.1 us
    dot_general x4, matrix products, block_scores(): jnp.einsum('qhd,khd->hqk', q_block, keys, preferred_element_type=jnp.floa...  37 us
    dot_general x2, matrix products, backward_pass(): jnp.einsum('qhd,khd->hqk', grad_block, values, preferred_element_type=jnp...  30.1 us
  transfers between devices with their start and end apart: 3, of which 3 were waited for; matrix products, arithmetic and copies ran while one was open for 6% of the time, Pallas kernels for 0%

commit v1 on v0

v1 whole, which is shorter than its diff:
```python
import jax
import jax.numpy as jnp
from jax import lax
from jax.experimental import pallas as pl
from jax.experimental.pallas import tpu as pltpu
from jax.sharding import PartitionSpec as P

SP = 1024
W = 768
NP = 6
EPS = 1e-05
NEG=-1e30
f32 = jnp.float32
bf16 = jnp.bfloat16
def tdot(a,b): return lax.dot_general(a,b,(((1,),(1,)),((),())),preferred_element_type=f32)
def dot(a,b): return jnp.dot(a,b,preferred_element_type=f32)
def head_masks():
    lane=lax.broadcasted_iota(jnp.int32,(1,128),1)
    return [lane<64, lane>=64]
def softmax_t(s):
    m=jnp.max(s,0,keepdims=True)
    p=jnp.exp(s-m)
    l=jnp.sum(p,0,keepdims=True)
    return m,l,p.astype(bf16)
DQ=256
def diag_fwd(place_ref, klen_ref, q_ref,k_ref,v_ref,o_ref,l_ref):
    hm=head_masks(); klen=klen_ref[0]
    q=q_ref[...]*jnp.asarray(0.125,bf16)
    vt=v_ref[...].T
    z=jnp.zeros((),bf16)
    tiles=[(qi,h) for qi in range(SP//DQ) for h in range(2)]
    kpos=lax.broadcasted_iota(jnp.int32,(SP,1),0)
    low=jnp.where(kpos<klen,kpos,SP)
    def scores(t):
        qi,h=t; n=(qi+1)*DQ
        ok=(qi*DQ+lax.broadcasted_iota(jnp.int32,(n,DQ),1))>=low[:n]
        return jnp.where(ok,tdot(k_ref[:n],jnp.where(hm[h],q[qi*DQ:n],z)),NEG)
    def finish(t,m,l,p):
        qi,h=t; n=(qi+1)*DQ; sl=slice(qi*DQ,n)
        acc=dot(vt[h*64:(h+1)*64,:n],p)
        o_ref[0,h*64:(h+1)*64,sl]=acc*(1.0/l)
        l_ref[0,h:h+1,sl]=m+jnp.log(l)
    pipeline(tiles,scores,softmax_t,finish)
def pipeline(tiles,scores,mid,finish,depth=2):
    s=scores(tiles[0]); pend=None
    for i,t in enumerate(tiles):
        sn=scores(tiles[i+1]) if i+1<len(tiles) else None
        r=mid(s) if not isinstance(s,tuple) else mid(t,*s)
        if depth==2:
            if pend: finish(*pend)
            pend=(t,)+r
        else: finish(t,*r)
        s=sn
    if pend: finish(*pend)
CQ=512
def cross_fwd(place_ref, klen_ref, q_ref,k_ref,v_ref,od_ref,ld_ref,o_ref,l_ref):
    hm=head_masks()
    @pl.when(place_ref[0]==1)
    def _():
        q=q_ref[...]*jnp.asarray(0.125,bf16)
        vt=v_ref[...].T
        z=jnp.zeros((),bf16)
        tiles=[(qi,h) for qi in range(SP//CQ) for h in range(2)]
        res={}
        def scores(t):
            qi,h=t
            return tdot(k_ref[...],jnp.where(hm[h],q[qi*CQ:(qi+1)*CQ],z))
        def finish(t,m,l,p):
            qi,h=t; sl=slice(qi*CQ,(qi+1)*CQ)
            acc=dot(vt[h*64:(h+1)*64],p)
            ld=ld_ref[0,h:h+1,sl]
            lx=m+jnp.log(l)
            mx=jnp.maximum(ld,lx)
            ed=jnp.exp(ld-mx); ex=jnp.exp(lx-mx); tot=ed+ex
            l_ref[0,h:h+1,sl]=mx+jnp.log(tot)
            res[t]=od_ref[0,h*64:(h+1)*64,sl]*(ed/tot)+acc*(ex/(tot*l))
            if h==1: o_ref[sl]=jnp.concatenate([res[(qi,0)],res[(qi,1)]],0).T.astype(bf16)
        pipeline(tiles,scores,softmax_t,finish)
    @pl.when(place_ref[0]==0)
    def _():
        o_ref[...]=od_ref[0].T.astype(bf16)
        l_ref[...]=ld_ref[...]
KB=256
def bwd_prep(q_ref,do_ref,hm):
    q=q_ref[...]*jnp.asarray(0.125,bf16)
    z=jnp.zeros((),bf16)
    do=do_ref[...]
    return [jnp.where(hm[h],q,z) for h in range(2)],[jnp.where(hm[h],do,z) for h in range(2)]
def bwd_tiles(k_ref,v_ref,qm,dm,lrow,drow,dk_ref,dv_ref,dqt,start,mask):
    tiles=[(kb,h) for kb in range(SP//KB) for h in range(2)]
    acc={}
    kts={}
    def scores(t):
        kb,h=t; ks=slice(kb*KB,(kb+1)*KB); q0=start(kb)
        return tdot(k_ref[ks],qm[h][q0:]),tdot(v_ref[ks],dm[h][q0:])
    def mid(t,s,dp):
        kb,h=t; q0=start(kb)
        p=jnp.exp(s-lrow(h)[:,q0:])
        if mask is not None: p=jnp.where(mask(kb),p,0.0)
        ds=p*(dp-drow(h)[:,q0:])
        return p.astype(bf16),ds.astype(bf16)
    def finish(t,p,ds):
        kb,h=t; ks=slice(kb*KB,(kb+1)*KB); q0=start(kb)
        if h==0: kts[kb]=k_ref[ks].T
        a=dot(p,dm[h][q0:]); b=dot(ds,qm[h][q0:])
        if h==0: acc[kb]=(a,b)
        else:
            dv_ref[ks]=(acc[kb][0]+a).astype(bf16); dk_ref[ks]=(acc[kb][1]+b).astype(bf16)
        c=dot(kts[kb][h*64:(h+1)*64],ds)
        if kb==0: dqt[h*64:(h+1)*64]=c
        else: dqt[h*64:(h+1)*64,q0:]+=c
    pipeline(tiles,scores,mid,finish)
def cross_bwd(place_ref, klen_ref, q_ref,k_ref,v_ref,do_ref,o_ref,l_ref,dq_ref,dk_ref,dv_ref,dl_ref,dqt):
    hm=head_masks()
    prod=do_ref[...].astype(f32)*o_ref[...].astype(f32)
    t=prod.T
    dl_ref[0,0:1]=jnp.sum(t[:64],0,keepdims=True); dl_ref[0,1:2]=jnp.sum(t[64:],0,keepdims=True)
    @pl.when(place_ref[0]==1)
    def _():
        qm,dm=bwd_prep(q_ref,do_ref,hm)
        bwd_tiles(k_ref,v_ref,qm,dm,lambda h:l_ref[0,h:h+1],lambda h:dl_ref[0,h:h+1],dk_ref,dv_ref,dqt,lambda kb:0,None)
        dq_ref[...]=dqt[...].T*0.125
    @pl.when(place_ref[0]==0)
    def _():
        dk_ref[...]=jnp.zeros_like(dk_ref); dv_ref[...]=jnp.zeros_like(dv_ref); dq_ref[...]=jnp.zeros_like(dq_ref)
def diag_bwd(place_ref, klen_ref, q_ref,k_ref,v_ref,do_ref,l_ref,dl_ref,dqx_ref,dq_ref,dk_ref,dv_ref,dqt):
    hm=head_masks(); klen=klen_ref[0]
    qm,dm=bwd_prep(q_ref,do_ref,hm)
    kpos=lax.broadcasted_iota(jnp.int32,(SP,1),0)
    low=jnp.where(kpos<klen,kpos,SP)
    def mask(kb):
        q0=kb*KB
        return q0+lax.broadcasted_iota(jnp.int32,(KB,SP-q0),1)>=low[q0:q0+KB]
    bwd_tiles(k_ref,v_ref,qm,dm,lambda h:l_ref[0,h:h+1],lambda h:dl_ref[0,h:h+1],dk_ref,dv_ref,dqt,lambda kb:kb*KB,mask)
    dq_ref[...]=(dqt[...].T*0.125+dqx_ref[...]).astype(bf16)
def col(base): return pl.BlockSpec((SP,128),lambda j,*_:(0,base+j))
ROW=pl.BlockSpec((1,8,SP),lambda j,*_:(j,0,0))
def call(fn,place,klen,ins,in_specs,outs,out_specs,scratch=(),flops=0):
    return pl.pallas_call(fn,
        grid_spec=pltpu.PrefetchScalarGridSpec(num_scalar_prefetch=2,grid=(NP,),in_specs=in_specs,out_specs=out_specs,scratch_shapes=list(scratch)),
        out_shape=outs,
        compiler_params=pltpu.CompilerParams(vmem_limit_bytes=50*1024*1024,dimension_semantics=("arbitrary",)),
        cost_estimate=pl.CostEstimate(flops=flops,bytes_accessed=10**7,transcendentals=10**7),
        name=fn.__name__,
    )(place,klen,*ins)
S=jax.ShapeDtypeStruct
def fwd(place,klen,qkv,kvr):
    c=col(0)
    T=pl.BlockSpec((1,128,SP),lambda j,*_:(j,0,0))
    od,ld=call(diag_fwd,place,klen,(qkv,qkv,qkv),[c,col(6),col(12)],[S((NP,128,SP),f32),S((NP,8,SP),f32)],[T,ROW])
    o,l=call(cross_fwd,place,klen,(qkv,kvr,kvr,od,ld),[c,c,col(6),T,ROW],[S((SP,W),bf16),S((NP,8,SP),f32)],[c,ROW])
    return o,l
def bwd(place,klen,qkv,kvr,do,o,l):
    c=col(0)
    acc=pltpu.VMEM((128,SP),f32)
    dqx,dkr,dvr,dl=call(cross_bwd,place,klen,(qkv,kvr,kvr,do,o,l),[c,c,col(6),c,c,ROW],
        [S((SP,W),f32),S((SP,W),bf16),S((SP,W),bf16),S((NP,8,SP),f32)],[c,c,c,ROW],[acc])
    dq,dk,dv=call(diag_bwd,place,klen,(qkv,qkv,qkv,do,l,dl,dqx),[c,col(6),col(12),c,ROW,ROW,c],[S((SP,W),bf16)]*3,[c,c,c],[acc])
    return dq,dk,dv,dkr,dvr


def swap_spans(x):
    return lax.ppermute(x, "blk", [(0, 1), (1, 0)])


def normalize(values, gain, shift):
    centered = values - jnp.mean(values, -1, keepdims=True)
    inv_std = lax.rsqrt(jnp.mean(centered * centered, -1, keepdims=True) + EPS)
    x_hat = centered * inv_std
    return x_hat * gain + shift, x_hat, inv_std


def norm_back(upstream, x_hat, inv_std, gain):
    scaled = upstream * gain
    inner = (
        scaled
        - jnp.mean(scaled, -1, keepdims=True)
        - x_hat * jnp.mean(scaled * x_hat, -1, keepdims=True)
    )
    return inv_std * inner, jnp.sum(upstream * x_hat, 0), jnp.sum(upstream, 0)


def rows_dot(left, right):
    return lax.dot_general(left, right, (((0,), (0,)), ((), ())), preferred_element_type=f32)


def body(
    inputs, cotangent, lengths, groups, flip,
    w_qkv, b_query, b_value, w_out, b_out, gain_one, shift_one, gain_two, shift_two,
    w_fc, b_fc, w_proj, b_proj,
):
    place = jnp.bitwise_xor(lax.axis_index("blk"), flip[0])
    klen = jnp.minimum(lengths[0] - place * SP, SP)
    place_s = place.reshape(1).astype(jnp.int32)
    klen_s = klen.reshape(1).astype(jnp.int32)
    x_b = inputs[0, 0]
    up_b = cotangent[0, 0]
    xr_b = swap_spans(x_b)

    x_in = x_b.astype(f32)
    normed_f, x_hat_one, inv_one = normalize(x_in, gain_one, shift_one)
    normed = normed_f.astype(bf16)
    qkv_bias = jnp.concatenate([b_query, jnp.zeros_like(b_value), b_value])
    qkv = (dot(normed, w_qkv) + qkv_bias).astype(bf16)
    c = col(0)
    tall = pl.BlockSpec((1, 128, SP), lambda j, *_: (j, 0, 0))
    od, ld = call(
        diag_fwd, place_s, klen_s, (qkv, qkv, qkv), [c, col(6), col(12)],
        [S((NP, 128, SP), f32), S((NP, 8, SP), f32)], [tall, ROW],
    )
    d_act = tdot(up_b, w_proj).astype(bf16)

    normed_r = normalize(xr_b.astype(f32), gain_one, shift_one)[0].astype(bf16)
    kvr = (dot(normed_r, w_qkv[:, W:]) + qkv_bias[W:]).astype(bf16)
    attended, lse = call(
        cross_fwd, place_s, klen_s, (qkv, kvr, kvr, od, ld), [c, c, col(6), tall, ROW],
        [S((SP, W), bf16), S((NP, 8, SP), f32)], [c, ROW],
    )

    branch_att = dot(attended, w_out) + b_out
    middle = x_in + branch_att
    normed_two_f, x_hat_two, inv_two = normalize(middle, gain_two, shift_two)
    normed_two = normed_two_f.astype(bf16)
    pre_act = dot(normed_two, w_fc) + b_fc
    gelu_val, gelu_back = jax.vjp(lambda val: jax.nn.gelu(val, approximate=True), pre_act)
    activ = gelu_val.astype(bf16)
    branch_mlp = dot(activ, w_proj) + b_proj
    outputs = middle + branch_mlp
    upstream = up_b.astype(f32)
    grad_pre = gelu_back(d_act.astype(f32))[0].astype(bf16)
    grad_w_proj = rows_dot(activ, up_b).astype(bf16)
    grad_w_fc = rows_dot(normed_two, grad_pre).astype(bf16)
    grad_mid_norm, grad_gain_two, grad_shift_two = norm_back(
        tdot(grad_pre, w_fc), x_hat_two, inv_two, gain_two
    )
    grad_middle = upstream + grad_mid_norm
    grad_att = grad_middle.astype(bf16)
    grad_w_out = rows_dot(attended, grad_att).astype(bf16)
    grad_attended = tdot(grad_att, w_out).astype(bf16)
    early = lax.psum((grad_w_proj, grad_w_fc, grad_w_out), ("blk", "dp"))

    acc = pltpu.VMEM((128, SP), f32)
    dqx, dkr, dvr, delta = call(
        cross_bwd, place_s, klen_s, (qkv, kvr, kvr, grad_attended, attended, lse),
        [c, c, col(6), c, c, ROW],
        [S((SP, W), f32), S((SP, W), bf16), S((SP, W), bf16), S((NP, 8, SP), f32)],
        [c, c, c, ROW], [acc],
    )
    w_q, w_k, w_v = w_qkv[:, :W], w_qkv[:, W : 2 * W], w_qkv[:, 2 * W :]
    returned = swap_spans((tdot(dkr, w_k) + tdot(dvr, w_v)).astype(bf16))
    dq, dk, dv = call(
        diag_bwd, place_s, klen_s, (qkv, qkv, qkv, grad_attended, lse, delta, dqx),
        [c, col(6), col(12), c, ROW, ROW, c], [S((SP, W), bf16)] * 3, [c, c, c], [acc],
    )
    grad_w_q = rows_dot(normed, dq).astype(bf16)
    grad_w_k = (rows_dot(normed, dk) + rows_dot(normed_r, dkr)).astype(bf16)
    grad_w_v = (rows_dot(normed, dv) + rows_dot(normed_r, dvr)).astype(bf16)
    late = lax.psum((grad_w_q, grad_w_k, grad_w_v), ("dp", "blk"))
    grad_b_query = jnp.sum(dq.astype(f32), 0)
    grad_b_value = jnp.sum(dv.astype(f32), 0) + jnp.sum(dvr.astype(f32), 0)

    grad_normed = tdot(dq, w_q) + tdot(dk, w_k) + tdot(dv, w_v) + returned.astype(f32)
    grad_x_norm, grad_gain_one, grad_shift_one = norm_back(
        grad_normed, x_hat_one, inv_one, gain_one
    )
    input_grad = (grad_middle + grad_x_norm).astype(bf16)

    valid = (jnp.arange(SP, dtype=jnp.int32) < klen).astype(f32)
    member = (groups[0] == jnp.arange(2, dtype=jnp.int32)).astype(f32)
    sums = jnp.stack(
        [jnp.sum(valid * jnp.sum(v * v, -1)) for v in (outputs, branch_att, branch_mlp)]
        + [jnp.sum(valid)]
    )
    small = lax.psum(
        jnp.concatenate([
            grad_b_query, grad_b_value, jnp.sum(grad_att.astype(f32), 0),
            grad_gain_one, grad_shift_one, grad_gain_two, grad_shift_two,
            jnp.sum(grad_pre.astype(f32), 0), jnp.sum(upstream, 0),
            (member[:, None] * sums[None, :]).reshape(-1),
        ]),
        ("dp", "blk"),
    )
    sizes = [W] * 7 + [4 * W, W]
    pieces = []
    at = 0
    for size in sizes:
        pieces.append(small[at : at + size])
        at += size
    table = small[at : at + 8].reshape(2, 4)
    group_rms = jnp.sqrt(table[:, :3] / (table[:, 3:] * W))
    g_bq, g_bv, g_bo, g_g1, g_s1, g_g2, g_s2, g_bfc, g_bp = pieces
    return (
        outputs.astype(bf16)[None, None], input_grad[None, None],
        jnp.concatenate(late, 1).astype(f32), g_bq, g_bv, early[2].astype(f32), g_bo,
        g_g1, g_s1, g_g2, g_s2, early[1].astype(f32), g_bfc, early[0].astype(f32), g_bp, group_rms,
    )


def solution(mesh):
    span = P("dp", "blk", None, None)
    return jax.shard_map(
        body,
        mesh=mesh,
        in_specs=(span, span, P("dp"), P("dp"), P("dp")) + (P(),) * 13,
        out_specs=(span, span) + (P(),) * 14,
        check_vma=False,
    )
```

time: 1240 us -> 634 us (0.51)
  waiting for transfers between devices: 520 us -> 297 us
  starting transfers between devices: 219 us -> 50.4 us
  matrix products: 225 us -> 114 us
  local copies, waits for them, and re-layouts: 94.3 us -> 15 us
  Pallas kernels: 0 us -> 53.3 us
  other arithmetic: 90.5 us -> 37.5 us
  loops' own time: 24.4 us -> 0 us
    ppermute x2, starting transfers between devices: 219 us -> 50 us  [swap_spans(): return lax.ppermute(x, 'blk', [(0, 1), (1, 0)])]
    ppermute x2, waiting for transfers between devices: 167 us -> 39.5 us  [swap_spans(): return lax.ppermute(x, 'blk', [(0, 1), (1, 0)])]
    dot_general x26 -> x21, matrix products: 225 us -> 114 us  [the longest x5 41.3 us: dot(): return jnp.dot(a, b, preferred_element_type=f32)]
    psum x1 -> x2, waiting for transfers between devices: 353 us -> 258 us  [the longest x1 219 us: body(): early = lax.psum((grad_w_proj, grad_w_fc, grad_w_out), ('blk', 'dp'))]
    pallas_call x0 -> x4, Pallas kernels: none -> 53.3 us  [call(): pl.pallas_call(fn, grid_spec=pltpu.PrefetchScalarGridSpec(num_scalar_pref...]
    unnamed x152 -> x88, local copies, waits for them, and re-layouts: 46.3 us -> 9.96 us
    reduce_sum x8 -> x7, other arithmetic: 32.3 us -> 5.86 us  [the longest x2 1.99 us: body(): grad_b_value = jnp.sum(dv.astype(f32), 0) + jnp.sum(dvr.astype(f32), 0)]
    slice x11 -> x3, local copies, waits for them, and re-layouts: 25.3 us -> 1.23 us  [the longest x2 1.23 us: body(): pieces.append(small[at:at + size])]
  transfers between devices with their start and end apart: 3 -> 4, of which waited for: 3 -> 4; matrix products, arithmetic and copies ran while one was open for 6% -> 7% of each run, Pallas kernels for 0% -> 2%
where the time goes in v1:
time: 634 us; the launch traced here: 625 us
  waiting for transfers between devices  297 us (47%)
  matrix products  114 us (18%)
  Pallas kernels  53.3 us (8%)
  starting transfers between devices  50.4 us (8%)
  blocking collectives  39.9 us (6%)
  other arithmetic  37.5 us (6%)
  between operations  16.9 us (3%)
  local copies, waits for them, and re-layouts  15 us (2%)
    psum x1, waiting for transfers between devices, body(): early = lax.psum((grad_w_proj, grad_w_fc, grad_w_out), ('blk', 'dp'))  219 us
    pallas_call x4, Pallas kernels, call(): pl.pallas_call(fn, grid_spec=pltpu.PrefetchScalarGridSpec(num_scalar_pref...  53.3 us
    ppermute x2, starting transfers between devices, swap_spans(): return lax.ppermute(x, 'blk', [(0, 1), (1, 0)])  50 us
    dot_general x5, matrix products, dot(): return jnp.dot(a, b, preferred_element_type=f32)  41.3 us
    dot_general x8, matrix products, tdot(): lax.dot_general(a, b, (((1,), (1,)), ((), ())), preferred_element_type=f32)  40.3 us
    psum x1, blocking collectives, body(): lax.psum(jnp.concatenate([grad_b_query, grad_b_value, jnp.sum(grad_att.as...  39.9 us
    ppermute x2, waiting for transfers between devices, swap_spans(): return lax.ppermute(x, 'blk', [(0, 1), (1, 0)])  39.5 us
    psum x1, waiting for transfers between devices, body(): late = lax.psum((grad_w_q, grad_w_k, grad_w_v), ('dp', 'blk'))  38.5 us
  transfers between devices with their start and end apart: 4, of which 4 were waited for; matrix products, arithmetic and copies ran while one was open for 7% of the time, Pallas kernels for 2%

profile of v1, /device:TPU:0, one launch (start us, length us, event | category | flops | bytes accessed | tf_op | source)
XLA Modules:
  0.0 624.8 jit_solution(11819719623831767322)
XLA Ops:
  9.1 3.0 collective-permute-start
  17.5 7.8 %add_convert_fusion.q_ref.k_ref.v_ref = bf16[1024,2304]{1,0:T(8,128)(2,1)} fusion(bf16[768,2304]{1,0:T(8,128)(2,1)} %param.23, f32[2304]{0:T(1024)S(1)} %pad_maximum_fusion, f32[768]{0:T(1024)S(1)} %copy-done.30, f32[768]{0:T(1024)S(1)} %copy-done.21, f32[1024]{0:T(1024)S(1)} %add_rsqrt_fusion.2, f32[1024]{0:T(1024)S(1)} %broadcast_multiply_fusion.6, ...), kind=kOutput, calls=%fused_computation.16 | convolution fusion | flops 3633315840 | bytes 9853952 | tf_op jit(solution)/shard_map/dot_general | solution.py:16
  25.3 14.6 %diag_fwd.1 = (f32[6,128,1024]{2,1,0:T(8,128)S(1)}, f32[6,8,1024]{2,1,0:T(8,128)S(1)}) custom-call(s32[1]{0:T(128)} %bitcast.2.place_ref, s32[1]{0:T(128)} %bitcast.4.klen_ref, bf16[1024,2304]{1,0:T(8,128)(2,1)} %add_convert_fusion.q_ref.k_ref.v_ref, bf16[1024,2304]{1,0:T(8,128)(2,1)} %add_convert_fusion.q_ref.k_ref.v_ref, ...), custom_call_target="tpu_custom_call" | custom-call | bytes 10000000 | tf_op jit(solution)/shard_map/diag_fwd/pallas_call | solution.py:139
  39.9 6.7 %collective-permute-done = bf16[1024,768]{0,1:T(8,128)(2,1)} collective-permute-done((bf16[1024,768]{0,1:T(8,128)(2,1)S(1)}, bf16[1024,768]{0,1:T(8,128)(2,1)}, u32[]{:S(2)}, u32[]{:S(2)}) %collective-permute-start) | collective-permute-done | bytes 1572896 | tf_op jit(solution)/shard_map/ppermute | solution.py:163
  50.2 6.1 add_convert_fusion.1.k_ref.v_ref
  56.3 5.5 cross_fwd.1
  65.0 12.9 %multiply_convert_fusion = (bf16[1024,3072]{1,0:T(8,128)(2,1)}, f32[1024,3072]{1,0:T(8,128)}) fusion(f32[3072]{0:T(1024)S(1)} %copy-done.26, bf16[768,3072]{1,0:T(8,128)(2,1)S(1)} %bitcast.68, f32[1024,768]{0,1:T(8,128)S(1)} %get-tuple-element.91, f32[768]{0:T(1024)S(1)} %copy-done.28, f32[768]{0:T(1024)S(1)} %copy-done.20, f32[1024]{0:T(1024)S(1)} %add_rsqrt_fusion, ...), kind=kOutput, calls=%fused_computation.15 | convolution fusion | flops 4867227648 | bytes 26765312 | tf_op jit(solution)/shard_map/dot_general | solution.py:16
  77.9 16.2 %convert_reduce_fusion = (f32[3072]{0:T(1024)S(1)}, bf16[1024,3072]{1,0:T(8,128)(2,1)}) fusion(f32[1024,3072]{1,0:T(8,128)} %get-tuple-element.104, f32[3072]{0:T(1024)S(1)} %copy-done.26, bf16[3072,768]{1,0:T(8,128)(2,1)S(1)} %bitcast.70, bf16[1,1,1024,768]{3,2,1,0:T(8,128)(2,1)S(1)} %copy-done.15), kind=kOutput, calls=%fused_computation.14 | convolution fusion | flops 4910478336 | bytes 25190400 | tf_op jit(solution)/shard_map/dot_general | solution.py:15
  94.0 9.3 %fusion.57 = (f32[768]{0:T(1024)S(1)}, f32[1024,768]{1,0:T(8,128)}) fusion(bf16[1024,3072]{1,0:T(8,128)(2,1)} %get-tuple-element.109, bf16[768,3072]{1,0:T(8,128)(2,1)S(1)} %bitcast.68), kind=kOutput, calls=%fused_computation.122 | convolution fusion | flops 4832623616 | bytes 14158848 | tf_op jit(solution)/shard_map/dot_general | solution.py:15
  103.4 7.0 %convolution_convert_fusion.1 = bf16[768,3072]{1,0:T(8,128)(2,1)} fusion(bf16[1024,3072]{1,0:T(8,128)(2,1)S(1)} %copy-done.31, f32[1024,768]{0,1:T(8,128)S(1)} %get-tuple-element.91, f32[768]{0:T(1024)S(1)} %copy-done.28, f32[768]{0:T(1024)S(1)} %copy-done.20, f32[1024]{0:T(1024)S(1)} %add_rsqrt_fusion, f32[1024]{0:T(1024)S(1)} %broadcast_multiply_fusion.4), kind=kOutput, calls=%fused_computation.19 | convolution fusion | flops 4838129664 | bytes 14170112 | tf_op jit(solution)/shard_map/dot_general | solution.py:184
  110.4 3.6 copy.47
  114.0 12.7 %multiply_reduce_fusion.2 = (f32[1024]{0:T(1024)S(1)}, f32[1024]{0:T(1024)S(1)}, f32[1024]{0:T(1024)S(1)}, f32[1024]{0:T(1024)S(1)}, f32[768]{0:T(1024)S(1)}, /*index=5*/bf16[1,1,1024,768]{2,3,1,0:T(8,128)(2,1)}) fusion(f32[1024,768]{0,1:T(8,128)} %copy-done.10, f32[768]{0:T(1024)S(1)} %copy-done.29, f32[1024,768]{0,1:T(8,128)} %copy.47, ...), kind=kOutput, calls=%fused_computation.51 | convolution fusion | flops 4843629568 | bytes 18908160 | tf_op jit(solution)/shard_map/dot_general | solution.py:16
  135.5 7.0 %cross_bwd.1 = (f32[1024,768]{1,0:T(8,128)}, bf16[1024,768]{1,0:T(8,128)(2,1)S(1)}, bf16[1024,768]{1,0:T(8,128)(2,1)S(1)}, f32[6,8,1024]{2,1,0:T(8,128)S(1)}) custom-call(s32[1]{0:T(128)} %bitcast.2.place_ref, s32[1]{0:T(128)} %bitcast.4.klen_ref, bf16[1024,2304]{1,0:T(8,128)(2,1)} %add_convert_fusion.q_ref.k_ref.v_ref, ...), custom_call_target="tpu_custom_call" | custom-call | bytes 10000000 | tf_op jit(solution)/shard_map/cross_bwd/pallas_call | solution.py:139
  142.5 26.3 %diag_bwd.1 = (bf16[1024,768]{1,0:T(8,128)(2,1)S(1)}, bf16[1024,768]{1,0:T(8,128)(2,1)S(1)}, bf16[1024,768]{1,0:T(8,128)(2,1)}) custom-call(s32[1]{0:T(128)} %bitcast.2.place_ref, s32[1]{0:T(128)} %bitcast.4.klen_ref, bf16[1024,2304]{1,0:T(8,128)(2,1)} %add_convert_fusion.q_ref.k_ref.v_ref, bf16[1024,2304]{1,0:T(8,128)(2,1)} %add_convert_fusion.q_ref.k_ref.v_ref, ...), custom_call_target="tpu_custom_call" | custom-call | bytes 10000000 | tf_op jit(solution)/shard_map/diag_bwd/pallas_call | solution.py:139
  168.8 2.7 convolution_convert_fusion.4
  176.5 2.7 pad_maximum_fusion.1
  179.3 2.7 add_convert_fusion.2
  181.9 4.1 add_convert_fusion.5
  186.1 4.1 add_convert_fusion.4
  190.5 9.1 %convolution_convert_fusion = bf16[3072,768]{1,0:T(8,128)(2,1)} fusion(bf16[1024,3072]{1,0:T(8,128)(2,1)} %get-tuple-element.103, bf16[1,1,1024,768]{3,2,1,0:T(8,128)(2,1)} %param.19), kind=kOutput, calls=%fused_computation.18 | convolution fusion | flops 4834197504 | bytes 12582912 | tf_op jit(solution)/shard_map/dot_general | solution.py:184
  202.6 47.0 %collective-permute-start.1 = (bf16[1024,768]{0,1:T(8,128)(2,1)}, bf16[1024,768]{0,1:T(8,128)(2,1)S(1)}, u32[]{:S(2)}, u32[]{:S(2)}) collective-permute-start(bf16[1024,768]{0,1:T(8,128)(2,1)} %add_convert_fusion.2), channel_id=1, source_target_pairs={{0,1},{1,0},{2,3},{3,2},{4,5},{5,4},{6,7},{7,6},{8,9},{9,8},{10,11... | collective-permute-start | bytes 4718600 | tf_op jit(solution)/shard_map/ppermute | solution.py:163
  251.6 2.9 fusion.35
  256.0 32.8 %collective-permute-done.1 = bf16[1024,768]{0,1:T(8,128)(2,1)S(1)} collective-permute-done((bf16[1024,768]{0,1:T(8,128)(2,1)}, bf16[1024,768]{0,1:T(8,128)(2,1)S(1)}, u32[]{:S(2)}, u32[]{:S(2)}) %collective-permute-start.1) | collective-permute-done | bytes 1572896 | tf_op jit(solution)/shard_map/ppermute | solution.py:163
  288.8 3.9 fusion.25
  292.8 39.9 %psum.52 = f32[9224]{0:T(1024)S(1)} all-reduce(f32[9224]{0:T(1024)S(1)} %constant_dynamic-update-slice_fusion), channel_id=1, replica_groups=mesh['dp'=16,'blk'=2] {'dp','blk'}, use_global_device_ids=true, to_apply=%region_30.0 | all-reduce | flops 9224 | bytes 73792 | tf_op jit(solution)/shard_map/psum | solution.py:274
  333.4 3.9 fusion.32
  340.3 38.5 %all-reduce.6.cloned.1.call-done = (bf16[768,768]{1,0:T(8,128)(2,1)}, bf16[768,768]{1,0:T(8,128)(2,1)}, bf16[768,768]{1,0:T(8,128)(2,1)}) async-done(((bf16[768,768]{1,0:T(8,128)(2,1)}, bf16[768,768]{1,0:T(8,128)(2,1)}, bf16[768,768]{1,0:T(8,128)(2,1)}), (bf16[768,768]{1,0:T(8,128)(2,1)}, bf16[768,768]{1,0:T(8,128)(2,1)}, bf16[768,768]{1,0:T(8,128)(2,1)})) %all-reduce.6.cloned.1.call-update) | async-done | bytes 3538960 | tf_op jit(solution)/shard_map/psum | solution.py:258
  378.8 4.6 maximum_convert_fusion
  383.4 219.2 %all-reduce.8.cloned.1.call-done = (bf16[768,768]{1,0:T(8,128)(2,1)}, bf16[768,3072]{1,0:T(8,128)(2,1)}, bf16[3072,768]{1,0:T(8,128)(2,1)}) async-done(((bf16[768,768]{1,0:T(8,128)(2,1)}, bf16[768,3072]{1,0:T(8,128)(2,1)}, bf16[3072,768]{1,0:T(8,128)(2,1)}), (bf16[768,768]{1,0:T(8,128)(2,1)}, bf16[768,3072]{1,0:T(8,128)(2,1)}, bf16[3072,768]{1,0:T(8,128)(2,1)})) %all-reduce.8.cloned.1.call-update) | async-done | bytes 10616848 | tf_op jit(solution)/shard_map/psum | solution.py:240
  602.6 3.0 convert_element_type.139
  605.6 7.4 %convert_element_type.141 = f32[768,3072]{1,0:T(8,128)} convert(bf16[768,3072]{1,0:T(8,128)(2,1)} %get-tuple-element.86) | non-fusion elementwise | flops 2359296 | bytes 14155776 | tf_op jit(solution)/shard_map/convert_element_type | solution.py:295
  613.0 4.5 convert_element_type.143
  (138 shorter events, 36.2 us)
Async XLA Ops:
  7.2 54.6 %copy-start = (bf16[768,768]{1,0:T(8,128)(2,1)S(1)}, bf16[768,768]{1,0:T(8,128)(2,1)}, u32[]{:S(2)}) copy-start(bf16[768,768]{1,0:T(8,128)(2,1)} %param.26) | copy-start | bytes 3538948
  7.2 5.2 copy-start.19
  7.2 5.2 copy-start.22
  7.2 371.6 %all-reduce.6.cloned.1.call-start = ((), (), s32[]{:S(2)}) async-start(), calls=%async_computation | async-start | bytes 7077888 | tf_op jit(solution)/shard_map/psum | solution.py:258
  9.1 8.4 %copy-start.6 = (bf16[1,1,1024,768]{2,3,1,0:T(8,128)(2,1)}, bf16[1,1,1024,768]{2,3,1,0:T(8,128)(2,1)S(1)}, u32[]{:S(2)}) copy-start(bf16[1,1,1024,768]{2,3,1,0:T(8,128)(2,1)S(1)} %copy.45) | copy-start | bytes 4718596
  9.1 8.4 %copy-start.21 = (f32[768]{0:T(1024)S(1)}, f32[768]{0:T(1024)}, u32[]{:S(2)}) copy-start(f32[768]{0:T(1024)} %param.28) | copy-start | bytes 9220
  9.1 8.4 %copy-start.30 = (f32[768]{0:T(1024)S(1)}, f32[768]{0:T(1024)}, u32[]{:S(2)}) copy-start(f32[768]{0:T(1024)} %param.29) | copy-start | bytes 9220
  9.1 37.5 %collective-permute-start = (bf16[1024,768]{0,1:T(8,128)(2,1)S(1)}, bf16[1024,768]{0,1:T(8,128)(2,1)}, u32[]{:S(2)}, u32[]{:S(2)}) collective-permute-start(bf16[1024,768]{0,1:T(8,128)(2,1)S(1)} %bitcast.64), channel_id=1, source_target_pairs={{0,1},{1,0},{2,3},{3,2},{4,5},{5,4},{6,7},{7,6},{8,9},{9,8},{10,11... | collective-permute-start | bytes 4718600 | tf_op jit(solution)/shard_map/ppermute | solution.py:163
  25.3 24.9 %copy-start.23 = (bf16[768,2304]{1,0:T(8,128)(2,1)S(1)}, bf16[768,2304]{1,0:T(8,128)(2,1)}, u32[]{:S(2)}) copy-start(bf16[768,2304]{1,0:T(8,128)(2,1)} %param.23) | copy-start | bytes 10616836
  39.9 16.4 %copy-start.4 = (f32[6,128,1024]{2,1,0:T(8,128)}, f32[6,128,1024]{2,1,0:T(8,128)S(1)}, u32[]{:S(2)}) copy-start(f32[6,128,1024]{2,1,0:T(8,128)S(1)} %get-tuple-element.27.od_ref) | copy-start | bytes 9437188
  56.3 5.5 copy-start.7
  56.3 5.5 copy-start.27
  61.8 67.4 %copy-start.5 = (bf16[1024,768]{1,0:T(8,128)(2,1)}, bf16[1024,768]{1,0:T(8,128)(2,1)S(1)}, u32[]{:S(2)}) copy-start(bf16[1024,768]{1,0:T(8,128)(2,1)S(1)} %get-tuple-element.29.o_ref) | copy-start | bytes 4718596
  63.7 39.7 %copy-start.10 = (f32[1024,768]{0,1:T(8,128)}, f32[1024,768]{0,1:T(8,128)S(1)}, u32[]{:S(2)}) copy-start(f32[1024,768]{0,1:T(8,128)S(1)} %get-tuple-element.91) | copy-start | bytes 9437188
  63.7 14.1 %slice-start.4 = ((s8[4718592]{0:T(1024)(128)(4,1)}), s8[4194304]{0:T(1024)(128)(4,1)S(1)}, s32[]{:S(2)}) async-start(s8[4718592]{0:T(1024)(128)(4,1)} %bitcast.69), calls=%async_computation.6 | async-start | bytes 8388608
  65.0 12.9 %copy-start.15 = (bf16[1,1,1024,768]{3,2,1,0:T(8,128)(2,1)S(1)}, bf16[1,1,1024,768]{3,2,1,0:T(8,128)(2,1)}, u32[]{:S(2)}) copy-start(bf16[1,1,1024,768]{3,2,1,0:T(8,128)(2,1)} %param.19) | copy-start | bytes 4718596
  65.0 12.9 %slice-start.5 = ((s8[4718592]{0:T(1024)(128)(4,1)}), s8[524288]{0:T(1024)(128)(4,1)S(1)}, s32[]{:S(2)}) async-start(s8[4718592]{0:T(1024)(128)(4,1)} %bitcast.69), calls=%async_computation.7 | async-start | bytes 1048576
  94.0 9.3 %copy-start.31 = (bf16[1024,3072]{1,0:T(8,128)(2,1)S(1)}, bf16[1024,3072]{1,0:T(8,128)(2,1)}, u32[]{:S(2)}) copy-start(bf16[1024,3072]{1,0:T(8,128)(2,1)} %get-tuple-element.109) | copy-start | bytes 18874372
  110.4 3.7 copy-start.29
  114.0 13.3 %copy-start.11 = (f32[1024,768]{0,1:T(8,128)S(1)}, f32[1024,768]{0,1:T(8,128)}, u32[]{:S(2)}) copy-start(f32[1024,768]{0,1:T(8,128)} %copy-done.10) | copy-start | bytes 9437188
  114.0 13.3 %copy-start.12 = (f32[1024,768]{0,1:T(8,128)S(1)}, f32[1024,768]{0,1:T(8,128)}, u32[]{:S(2)}) copy-start(f32[1024,768]{0,1:T(8,128)} %copy.47) | copy-start | bytes 9437188
  114.0 13.3 %copy-start.14 = (bf16[1,1,1024,768]{2,3,1,0:T(8,128)(2,1)S(1)}, bf16[1,1,1024,768]{2,3,1,0:T(8,128)(2,1)}, u32[]{:S(2)}) copy-start(bf16[1,1,1024,768]{2,3,1,0:T(8,128)(2,1)} %copy.46) | copy-start | bytes 4718596
  129.1 5.1 copy-start.13
  142.5 26.3 %copy-start.8 = (bf16[1,1,1024,768]{2,3,1,0:T(8,128)(2,1)S(1)}, bf16[1,1,1024,768]{2,3,1,0:T(8,128)(2,1)}, u32[]{:S(2)}) copy-start(bf16[1,1,1024,768]{2,3,1,0:T(8,128)(2,1)} %copy-done.6) | copy-start | bytes 4718596
  190.2 412.4 %all-reduce.8.cloned.1.call-start = ((), (), s32[]{:S(2)}) async-start(), calls=%async_computation.1 | async-start | bytes 21233664 | tf_op jit(solution)/shard_map/psum | solution.py:240
  199.6 50.0 %copy-start.18 = (f32[9224]{0:T(1024)S(1)}, f32[9224]{0:T(1024)}, u32[]{:S(2)}) copy-start(f32[9224]{0:T(1024)} %custom-call) | copy-start | bytes 110692
  202.6 86.2 %collective-permute-start.1 = (bf16[1024,768]{0,1:T(8,128)(2,1)}, bf16[1024,768]{0,1:T(8,128)(2,1)S(1)}, u32[]{:S(2)}, u32[]{:S(2)}) collective-permute-start(bf16[1024,768]{0,1:T(8,128)(2,1)} %add_convert_fusion.2), channel_id=1, source_target_pairs={{0,1},{1,0},{2,3},{3,2},{4,5},{5,4},{6,7},{7,6},{8,9},{9,8},{10,11... | collective-permute-start | bytes 4718600 | tf_op jit(solution)/shard_map/ppermute | solution.py:163
  254.5 34.2 %copy-start.9 = (bf16[1,1,1024,768]{2,3,1,0:T(8,128)(2,1)S(1)}, bf16[1,1,1024,768]{2,3,1,0:T(8,128)(2,1)}, u32[]{:S(2)}) copy-start(bf16[1,1,1024,768]{2,3,1,0:T(8,128)(2,1)} %copy-done.6) | copy-start | bytes 4718596
  254.5 34.2 %copy-start.17 = (bf16[1024,768]{1,0:T(8,128)(2,1)S(1)}, bf16[1024,768]{1,0:T(8,128)(2,1)}, u32[]{:S(2)}) copy-start(bf16[1024,768]{1,0:T(8,128)(2,1)} %get-tuple-element.35) | copy-start | bytes 4718596
  602.6 10.4 %slice-start = ((s8[4718592]{0:T(1024)(128)(4,1)}), s8[4194304]{0:T(1024)(128)(4,1)S(1)}, s32[]{:S(2)}) async-start(s8[4718592]{0:T(1024)(128)(4,1)} %bitcast.65), calls=%async_computation.2 | async-start | bytes 8388608
  605.6 7.4 %slice-start.1 = ((s8[4718592]{0:T(1024)(128)(4,1)}), s8[524288]{0:T(1024)(128)(4,1)S(1)}, s32[]{:S(2)}) async-start(s8[4718592]{0:T(1024)(128)(4,1)} %bitcast.65), calls=%async_computation.3 | async-start | bytes 1048576
  613.0 4.5 copy-start.1
  (10 other events, 21.3 us)
Sparse Core Ops, SparseCore 0:
  190.3 188.4 all-reduce.5
  386.9 215.6 all-reduce.7

commit v2 on v1

v2 whole, which is shorter than its diff:
```python
import jax
import jax.numpy as jnp
from jax import lax
from jax.experimental import pallas as pl
from jax.experimental.pallas import tpu as pltpu
from jax.sharding import PartitionSpec as P

SP = 1024
W = 768
NP = 6
EPS = 1e-05
NEG=-1e30
f32=jnp.float32; bf16=jnp.bfloat16
def tdot(a,b): return lax.dot_general(a,b,(((1,),(1,)),((),())),preferred_element_type=f32)
def dot(a,b): return jnp.dot(a,b,preferred_element_type=f32)
def head_masks():
    lane=lax.broadcasted_iota(jnp.int32,(1,128),1)
    return [lane<64, lane>=64]
def softmax_t(s):
    m=jnp.max(s,0,keepdims=True)
    p=jnp.exp(s-m)
    l=jnp.sum(p,0,keepdims=True)
    return m,l,p.astype(bf16)
DQ=256
def diag_fwd(place_ref, klen_ref, q_ref,k_ref,v_ref,o_ref,l_ref):
    hm=head_masks(); klen=klen_ref[0]
    q=q_ref[...]*jnp.asarray(0.125,bf16)
    vt=v_ref[...].T
    z=jnp.zeros((),bf16)
    tiles=[(qi,h) for qi in range(SP//DQ) for h in range(2)]
    kpos=lax.broadcasted_iota(jnp.int32,(SP,1),0)
    low=jnp.where(kpos<klen,kpos,SP)
    def scores(t):
        qi,h=t; n=(qi+1)*DQ
        ok=(qi*DQ+lax.broadcasted_iota(jnp.int32,(n,DQ),1))>=low[:n]
        return jnp.where(ok,tdot(k_ref[:n],jnp.where(hm[h],q[qi*DQ:n],z)),NEG)
    def finish(t,m,l,p):
        qi,h=t; n=(qi+1)*DQ; sl=slice(qi*DQ,n)
        acc=dot(vt[h*64:(h+1)*64,:n],p)
        o_ref[0,h*64:(h+1)*64,sl]=acc*(1.0/l)
        l_ref[0,h:h+1,sl]=m+jnp.log(l)
    pipeline(tiles,scores,softmax_t,finish)
def pipeline(tiles,scores,mid,finish,depth=2):
    s=scores(tiles[0]); pend=None
    for i,t in enumerate(tiles):
        sn=scores(tiles[i+1]) if i+1<len(tiles) else None
        r=mid(s) if not isinstance(s,tuple) else mid(t,*s)
        if depth==2:
            if pend: finish(*pend)
            pend=(t,)+r
        else: finish(t,*r)
        s=sn
    if pend: finish(*pend)
CQ=512
def cross_fwd(place_ref, klen_ref, q_ref,k_ref,v_ref,od_ref,ld_ref,o_ref,l_ref):
    hm=head_masks()
    @pl.when(place_ref[0]==1)
    def _():
        q=q_ref[...]*jnp.asarray(0.125,bf16)
        vt=v_ref[...].T
        z=jnp.zeros((),bf16)
        tiles=[(qi,h) for qi in range(SP//CQ) for h in range(2)]
        res={}
        def scores(t):
            qi,h=t
            return tdot(k_ref[...],jnp.where(hm[h],q[qi*CQ:(qi+1)*CQ],z))
        def finish(t,m,l,p):
            qi,h=t; sl=slice(qi*CQ,(qi+1)*CQ)
            acc=dot(vt[h*64:(h+1)*64],p)
            ld=ld_ref[0,h:h+1,sl]
            lx=m+jnp.log(l)
            mx=jnp.maximum(ld,lx)
            ed=jnp.exp(ld-mx); ex=jnp.exp(lx-mx); tot=ed+ex
            l_ref[0,h:h+1,sl]=mx+jnp.log(tot)
            res[t]=od_ref[0,h*64:(h+1)*64,sl]*(ed/tot)+acc*(ex/(tot*l))
            if h==1: o_ref[sl]=jnp.concatenate([res[(qi,0)],res[(qi,1)]],0).T.astype(bf16)
        pipeline(tiles,scores,softmax_t,finish)
    @pl.when(place_ref[0]==0)
    def _():
        o_ref[...]=od_ref[0].T.astype(bf16)
        l_ref[...]=ld_ref[...]
KB=256
def bwd_prep(q_ref,do_ref,hm):
    q=q_ref[...]*jnp.asarray(0.125,bf16)
    z=jnp.zeros((),bf16)
    do=do_ref[...]
    return [jnp.where(hm[h],q,z) for h in range(2)],[jnp.where(hm[h],do,z) for h in range(2)]
def bwd_tiles(k_ref,v_ref,qm,dm,lrow,drow,put,dqt,start,mask):
    tiles=[(kb,h) for kb in range(SP//KB) for h in range(2)]
    acc={}
    kts={}
    def scores(t):
        kb,h=t; ks=slice(kb*KB,(kb+1)*KB); q0=start(kb)
        return tdot(k_ref[ks],qm[h][q0:]),tdot(v_ref[ks],dm[h][q0:])
    def mid(t,s,dp):
        kb,h=t; q0=start(kb)
        p=jnp.exp(s-lrow(h)[:,q0:])
        if mask is not None: p=jnp.where(mask(kb),p,0.0)
        ds=p*(dp-drow(h)[:,q0:])
        return p.astype(bf16),ds.astype(bf16)
    def finish(t,p,ds):
        kb,h=t; ks=slice(kb*KB,(kb+1)*KB); q0=start(kb)
        if h==0: kts[kb]=k_ref[ks].T
        a=dot(p,dm[h][q0:]); b=dot(ds,qm[h][q0:])
        if h==0: acc[kb]=(a,b)
        else:
            put(ks,(acc[kb][1]+b).astype(bf16),(acc[kb][0]+a).astype(bf16))
        c=dot(kts[kb][h*64:(h+1)*64],ds)
        if kb==0: dqt[h*64:(h+1)*64]=c
        else: dqt[h*64:(h+1)*64,q0:]+=c
    pipeline(tiles,scores,mid,finish)
def cross_bwd(place_ref, klen_ref, q_ref,k_ref,v_ref,do_ref,o_ref,l_ref,dq_ref,dkv_ref,dl_ref,dqt):
    hm=head_masks()
    prod=do_ref[...].astype(f32)*o_ref[...].astype(f32)
    t=prod.T
    dl_ref[0,0:1]=jnp.sum(t[:64],0,keepdims=True); dl_ref[0,1:2]=jnp.sum(t[64:],0,keepdims=True)
    @pl.when(place_ref[0]==1)
    def _():
        def put(ks,dk,dv):
            dkv_ref[0,ks]=dk
            dkv_ref[1,ks]=dv
        qm,dm=bwd_prep(q_ref,do_ref,hm)
        bwd_tiles(k_ref,v_ref,qm,dm,lambda h:l_ref[0,h:h+1],lambda h:dl_ref[0,h:h+1],put,dqt,lambda kb:0,None)
        dq_ref[...]=dqt[...].T*0.125
    @pl.when(place_ref[0]==0)
    def _():
        dkv_ref[...]=jnp.zeros_like(dkv_ref); dq_ref[...]=jnp.zeros_like(dq_ref)
def diag_bwd(place_ref, klen_ref, q_ref,k_ref,v_ref,do_ref,l_ref,dl_ref,dqx_ref,out_ref,dqt):
    hm=head_masks(); klen=klen_ref[0]
    qm,dm=bwd_prep(q_ref,do_ref,hm)
    def put(ks,dk,dv):
        out_ref[1,ks]=dk
        out_ref[2,ks]=dv
    kpos=lax.broadcasted_iota(jnp.int32,(SP,1),0)
    low=jnp.where(kpos<klen,kpos,SP)
    def mask(kb):
        q0=kb*KB
        return q0+lax.broadcasted_iota(jnp.int32,(KB,SP-q0),1)>=low[q0:q0+KB]
    bwd_tiles(k_ref,v_ref,qm,dm,lambda h:l_ref[0,h:h+1],lambda h:dl_ref[0,h:h+1],put,dqt,lambda kb:kb*KB,mask)
    out_ref[0]=(dqt[...].T*0.125+dqx_ref[...]).astype(bf16)
S=jax.ShapeDtypeStruct
def col(base,rows=SP): return pl.BlockSpec((rows,128),lambda j,*_:(0,base+j))
def cols(n,base): return pl.BlockSpec((n,SP,128),lambda j,*_:(0,0,base+j))
def row(base): return pl.BlockSpec((1,8,SP),lambda j,*_:(base+j,0,0))
ROW=row(0)
def call(fn,place,klen,ins,in_specs,outs,out_specs,scratch=(),pairs=NP,into=None,after=(),flops=0,trans=0):
    into=into or {}
    extra=list(into.items())
    n=2+len(ins)
    m=len(extra)
    skip=n+m+len(after)
    def kern(*refs): return fn(*refs[:n],*refs[skip:])
    specs=list(in_specs)+[pl.BlockSpec(memory_space=pl.ANY)]*(m+len(after))
    return pl.pallas_call(kern,
        grid_spec=pltpu.PrefetchScalarGridSpec(num_scalar_prefetch=2,grid=(pairs,),in_specs=specs,out_specs=out_specs,scratch_shapes=list(scratch)),
        out_shape=outs,
        input_output_aliases={n+i:o for i,(o,_) in enumerate(extra)},
        compiler_params=pltpu.CompilerParams(vmem_limit_bytes=50*1024*1024,dimension_semantics=("arbitrary",)),
        cost_estimate=pl.CostEstimate(flops=flops,bytes_accessed=pairs*10**4,transcendentals=trans),
        name=fn.__name__,
    )(place,klen,*ins,*[x for _,x in extra],*after)


BITS = {"c": ("dp", 1), "y": ("dp", 2), "u": ("dp", 4), "v": ("dp", 8), "x": ("blk", 1)}
LOW = "xyuv"
ORDERS = ("xyuv", "yuxv", "uxyv")
RB = 48


def swap(a, bit):
    axis, step = BITS[bit] if isinstance(bit, str) else ("dp", bit)
    return lax.ppermute(a, axis, [(i, i ^ step) for i in range(lax.axis_size(axis))])


def outer_steps():
    size = lax.axis_size("dp")
    return [1 << k for k in range(4, 16) if (1 << k) < size]


def my_id():
    place = 0
    for bit in "c" + LOW:
        axis, step = BITS[bit]
        place = 2 * place + (lax.axis_index(axis) // step) % 2
    return place.astype(jnp.int32).reshape(1)


def add(a, b):
    return (a.astype(f32) + b.astype(f32)).astype(bf16)


def core_step(keeps, sends):
    state = []
    for keep, send in zip(keeps, sends):
        a = add(keep, swap(send, "c"))
        state.append((a.reshape((2,) * 4 + a.shape[1:]), LOW))
    return state


def low_step(state, step, after=None):
    waiting = []
    for (a, bits), order in zip(state, ORDERS):
        at = bits.index(order[step])
        keep, send = lax.index_in_dim(a, 0, at, False), lax.index_in_dim(a, 1, at, False)
        waiting.append((keep, swap(send, order[step]), bits.replace(order[step], "")))
    if after is not None:
        flat = lambda a: a.reshape(-1, a.shape[-1])
        sums = sum_kernel([(flat(keep), flat(got)) for keep, got, _ in waiting], after, "step_sum")
        return [(a.reshape(keep.shape), bits) for a, (keep, _, bits) in zip(sums, waiting)]
    return [(add(keep, got), bits) for keep, got, bits in waiting]


def sum_kernel(pairs, after, name):
    n = len(pairs)

    def kern(*refs):
        for i in range(n):
            refs[i - n][...] = add(refs[i][...], refs[n + i][...])

    vmem = pl.BlockSpec(memory_space=pltpu.VMEM)
    return pl.pallas_call(
        kern,
        in_specs=[vmem] * (2 * n) + [pl.BlockSpec(memory_space=pl.ANY)] * len(after),
        out_specs=[vmem] * n,
        out_shape=[S(a.shape, bf16) for a, _ in pairs],
        name=name,
    )(*[a for a, _ in pairs], *[b for _, b in pairs], *after)


def last_step(state, after):
    pairs = [(a[0], swap(a[1], order[3])) for (a, _), order in zip(state, ORDERS)]
    total = jnp.stack(sum_kernel(pairs, after, "last_sum"))
    for step in outer_steps():
        total = add(total, swap(total, step))
    return total


def outer_sum(blocks):
    for step in outer_steps():
        blocks = [add(a, swap(a, step)) for a in blocks]
    return blocks


def reduce_parts(keeps, sends):
    state = core_step(keeps, sends)
    for step in range(4):
        state = low_step(state, step)
    return outer_sum([a for a, _ in state])


def spread_parts(blocks):
    state = [a[None] for a in blocks]
    for step in (3, 2, 1, 0):
        state = [jnp.concatenate([a, swap(a, o[step])], 0) for a, o in zip(state, ORDERS)]
    return state, [swap(a, "c") for a in state]


def sum_small(a):
    for bit in "c" + LOW:
        a = a + swap(a, bit)
    for step in outer_steps():
        a = a + swap(a, step)
    return a


def low_index(p, order):
    r = 0
    for bit in order:
        r = 2 * r + (p // (1 << (3 - LOW.index(bit)))) % 2
    return r


def gather_all(blocks):
    a = lax.all_gather(blocks, ("dp", "blk"), axis=0, tiled=False)
    return a[:32]


def device_of(block):
    c, x, y, u, v = [(block // (1 << (4 - i))) % 2 for i in range(5)]
    return (v * 8 + u * 4 + y * 2 + c) * 2 + x


def unpack_early(gathered):
    rows = 2

    def kern(*refs):
        ins, (fc, proj, out) = refs[: 2 * rows], refs[2 * rows :]
        for core in range(2):
            for r in range(rows):
                a = ins[core * rows + r]
                at = slice(r * RB, (r + 1) * RB)
                fc[at, core * 1536 : core * 1536 + 1152] = a[0, 0].astype(f32)
                fc[at, core * 1536 + 1152 : (core + 1) * 1536] = a[0, 1, :, :384].astype(f32)
                proj[core, 2 * r * RB : (2 * r + 1) * RB] = a[0, 1, :, 384:].astype(f32)
                proj[core, (2 * r + 1) * RB : (2 * r + 2) * RB] = a[0, 2, :, :768].astype(f32)
                out[at, core * 384 : (core + 1) * 384] = a[0, 2, :, 768:].astype(f32)

    block = (1,) + gathered.shape[1:]
    return pl.pallas_call(
        kern,
        grid=(16 // rows,),
        in_specs=[
            pl.BlockSpec(block, lambda b, core=core, r=r: (device_of(core * 16 + b * rows + r), 0, 0, 0))
            for core in range(2) for r in range(rows)
        ],
        out_specs=[
            pl.BlockSpec((rows * RB, 4 * W), lambda b: (b, 0)),
            pl.BlockSpec((2, 2 * rows * RB, W), lambda b: (0, b, 0)),
            pl.BlockSpec((rows * RB, W), lambda b: (b, 0)),
        ],
        out_shape=[S((W, 4 * W), f32), S((2, 2 * W, W), f32), S((W, W), f32)],
        compiler_params=pltpu.CompilerParams(vmem_limit_bytes=56 * 1024 * 1024),
        cost_estimate=pl.CostEstimate(flops=0, bytes_accessed=3 * gathered.size * 2, transcendentals=0),
        name="unpack_early",
    )(*[gathered] * (2 * rows))


def unpack_late(me, mine, other):
    n = len(mine)
    rows = 4
    lanes = mine[0].shape[2]

    def kern(me_ref, *refs):
        own, far, out = refs[:n], refs[n : 2 * n], refs[-1]
        core, low = me_ref[0] // 16, me_ref[0] % 16
        step = pl.program_id(0)

        def fill(half, ins):
            for r in range(rows):
                place = (step * rows + r) ^ low
                for part in range(n):
                    at = (half * n + part) * lanes
                    out[r * RB : (r + 1) * RB, at : at + lanes] = ins[part][low_index(place, ORDERS[part])].astype(f32)

        for half in range(2):
            @pl.when(core == half)
            def _():
                fill(half, own)

            @pl.when(core != half)
            def _():
                fill(half, far)

    whole = pl.BlockSpec(mine[0].shape, lambda b, *_: (0, 0, 0))
    return pl.pallas_call(
        kern,
        grid_spec=pltpu.PrefetchScalarGridSpec(
            num_scalar_prefetch=1, grid=(16 // rows,), in_specs=[whole] * (2 * n),
            out_specs=pl.BlockSpec((rows * RB, 3 * W), lambda b, *_: (b, 0)),
        ),
        out_shape=S((W, 3 * W), f32),
        compiler_params=pltpu.CompilerParams(vmem_limit_bytes=56 * 1024 * 1024),
        cost_estimate=pl.CostEstimate(flops=0, bytes_accessed=10**7, transcendentals=0),
        name="unpack_late",
    )(me, *mine, *other)


MR = 256
FC = 768
C0 = 0.7978845608028654
C1 = C0 * 0.044715


def rowmean(a):
    return jnp.sum(a, -1, keepdims=True) * (1.0 / W)


def block_kernel(
    klen_ref, x_ref, att_ref, up_ref, w_out_ref, w_fc_ref, w_proj_ref, vec_ref, b_fc_ref,
    y_ref, act_ref, pre_ref, mid_ref, gatt_ref, do_ref, sums_ref, bsum_ref,
):
    step = pl.program_id(0)

    @pl.when(step == 0)
    def _():
        sums_ref[...] = jnp.zeros_like(sums_ref)
        bsum_ref[...] = jnp.zeros_like(bsum_ref)

    up_b = up_ref[...]
    up = up_b.astype(f32)
    branch_att = dot(att_ref[...], w_out_ref[...]) + vec_ref[0:1]
    middle = x_ref[...].astype(f32) + branch_att
    centered = middle - rowmean(middle)
    inv = lax.rsqrt(rowmean(centered * centered) + EPS)
    x_hat = centered * inv
    normed = (x_hat * vec_ref[1:2] + vec_ref[2:3]).astype(bf16)
    mid_ref[...] = normed
    chunks = range(4 * W // FC)
    sl = lambda c: slice(c * FC, (c + 1) * FC)

    def first(c):
        return dot(normed, w_fc_ref[:, sl(c)]), tdot(up_b, w_proj_ref[sl(c)])

    mlp = None
    back = None
    ahead = first(0)
    for c in chunks:
        u, dz = ahead
        if c + 1 < len(chunks):
            ahead = first(c + 1)
        u = u + b_fc_ref[0:1, sl(c)]
        v = u * u
        h = 0.5 + 0.5 * jnp.tanh(u * (C0 + C1 * v))
        z = (u * h).astype(bf16)
        d = dz * (h + (u * (2 * C0 + 6 * C1 * v)) * (h * (1.0 - h)))
        bsum_ref[0:1, sl(c)] += jnp.sum(d, 0, keepdims=True)
        d = d.astype(bf16)
        act_ref[:, sl(c)] = z
        pre_ref[:, sl(c)] = d
        a = dot(z, w_proj_ref[sl(c)])
        b = tdot(d, w_fc_ref[:, sl(c)])
        mlp = a if mlp is None else mlp + a
        back = b if back is None else back + b
    branch_mlp = mlp + vec_ref[3:4]
    out = middle + branch_mlp
    y_ref[...] = out.astype(bf16)
    scaled = back * vec_ref[1:2]
    grad = up + inv * (scaled - rowmean(scaled) - x_hat * rowmean(scaled * x_hat))
    gatt = grad.astype(bf16)
    gatt_ref[...] = gatt
    do_ref[...] = tdot(gatt, w_out_ref[...]).astype(bf16)
    valid = step * MR + lax.broadcasted_iota(jnp.int32, (MR, 1), 0) < klen_ref[0]
    total = lambda a: jnp.sum(a, 0, keepdims=True)
    kept = lambda a: total(jnp.where(valid, a * a, 0.0))
    sums_ref[...] += jnp.concatenate(
        [total(back * x_hat), total(back), total(grad), total(up), kept(out), kept(branch_att), kept(branch_mlp),
         jnp.zeros((1, W), f32)], 0,
    )


def block_call(klen, x, att, up, w_out, w_fc, w_proj, vec, b_fc):
    once = pl.Buffered(1)
    rows = lambda width: pl.BlockSpec((MR, width), lambda i, *_: (i, 0))
    whole = lambda shape: pl.BlockSpec(shape, lambda i, *_: (0, 0), pipeline_mode=once)
    const = lambda shape: pl.BlockSpec(shape, lambda i, *_: (0, 0))
    return pl.pallas_call(
        block_kernel,
        grid_spec=pltpu.PrefetchScalarGridSpec(
            num_scalar_prefetch=1,
            grid=(SP // MR,),
            in_specs=[rows(W)] * 3 + [whole((W, W)), whole((W, 4 * W)), whole((4 * W, W)), const((8, W)), const((1, 4 * W))],
            out_specs=[rows(W), rows(4 * W), rows(4 * W), rows(W), rows(W), rows(W), const((8, W)), const((1, 4 * W))],
        ),
        out_shape=[
            S((SP, W), bf16), S((SP, 4 * W), bf16), S((SP, 4 * W), bf16), S((SP, W), bf16),
            S((SP, W), bf16), S((SP, W), bf16), S((8, W), f32), S((1, 4 * W), f32),
        ],
        compiler_params=pltpu.CompilerParams(vmem_limit_bytes=56 * 1024 * 1024),
        cost_estimate=pl.CostEstimate(flops=22 * 10**9, bytes_accessed=35 * 10**6, transcendentals=3 * 10**6),
        name="block_mlp",
    )(klen, x, att, up, w_out, w_fc, w_proj, vec, b_fc)


def grads_kernel(me_ref, mid_ref, pre_ref, act_ref, up_ref, att_ref, gatt_ref, k0, k1, k2, s0, s1, s2, mid_t):
    step = pl.program_id(0)
    core, low = me_ref[0] // 16, me_ref[0] % 16

    @pl.when(step == 0)
    def _():
        mid_t[...] = mid_ref[...].T

    def by_core(half, fill, keep, send):
        @pl.when(half == core)
        def _():
            fill(*keep)

        @pl.when(half != core)
        def _():
            fill(*send)

    @pl.when(step < 4)
    def _():
        tile = dot(mid_t[...], pre_ref[...]).astype(bf16)

        def left(one):
            for i in range(16):
                one[i ^ low, :, :768] = tile[i * RB : (i + 1) * RB]

        def right(one, two):
            for i in range(16):
                one[i ^ low, :, 768:] = tile[i * RB : (i + 1) * RB, :384]
                two[i ^ low, :, :384] = tile[i * RB : (i + 1) * RB, 384:]

        @pl.when(step % 2 == 0)
        def _():
            by_core(step // 2, left, (k0,), (s0,))

        @pl.when(step % 2 == 1)
        def _():
            by_core(step // 2, right, (k0, k1), (s0, s1))

    @pl.when((step >= 4) & (step < 8))
    def _():
        tile = rows_dot(act_ref[...], up_ref[...]).astype(bf16)
        first = (step - 4) % 2 * 8

        def fill(one, two):
            for i in range(8):
                at = (first + i) ^ low
                one[at, :, 384:] = tile[2 * i * RB : (2 * i + 1) * RB]
                two[at, :, :768] = tile[(2 * i + 1) * RB : (2 * i + 2) * RB]

        by_core((step - 4) // 2, fill, (k1, k2), (s1, s2))

    @pl.when(step == 8)
    def _():
        tile = rows_dot(att_ref[...], gatt_ref[...]).astype(bf16)

        def fill(one, two):
            for i in range(16):
                one[i ^ low, :, 768:] = tile[i * RB : (i + 1) * RB, :384]
                two[i ^ low, :, 768:] = tile[i * RB : (i + 1) * RB, 384:]

        by_core(0, fill, (k2, s2), (s2, k2))


def grads_call(me, mid, pre, act, up, att, gatt):
    clip = lambda i, lo, hi: jnp.clip(i, lo, hi) - lo
    whole = pl.BlockSpec((SP, W), lambda i, *_: (0, 0))
    part = pl.BlockSpec((16, RB, 1152), lambda i, *_: (0, 0, 0))
    res = pl.pallas_call(
        grads_kernel,
        grid_spec=pltpu.PrefetchScalarGridSpec(
            num_scalar_prefetch=1,
            grid=(9,),
            in_specs=[
                whole,
                pl.BlockSpec((SP, W), lambda i, *_: (0, clip(i, 0, 3))),
                pl.BlockSpec((SP, W), lambda i, *_: (0, clip(i, 4, 7))),
                whole,
                whole,
                whole,
            ],
            out_specs=[part] * 6,
            scratch_shapes=[pltpu.VMEM((W, SP), bf16)],
        ),
        out_shape=[S((16, RB, 1152), bf16)] * 6,
        compiler_params=pltpu.CompilerParams(vmem_limit_bytes=56 * 1024 * 1024),
        cost_estimate=pl.CostEstimate(flops=11 * 10**9, bytes_accessed=30 * 10**6, transcendentals=0),
        name="block_grads",
    )(me, mid, pre, act, up, att, gatt)
    return res[:3], res[3:]


def late_kernel(me_ref, a_ref, ar_ref, d_ref, dr_ref, k0, k1, k2, s0, s1, s2, a_t, ar_t):
    step = pl.program_id(0)
    core, low = me_ref[0] // 16, me_ref[0] % 16

    def put(keep, send, tile):
        def fill(ref):
            for i in range(16):
                ref[i ^ low] = tile[i * RB : (i + 1) * RB]

        return lambda half: (
            pl.when(core == half)(lambda: fill(keep)),
            pl.when(core != half)(lambda: fill(send)),
        )

    @pl.when(step == 0)
    def _():
        a_t[...] = a_ref[...].T
        ar_t[...] = ar_ref[...].T
        tile = dot(a_t[...], d_ref[0]).astype(bf16)
        put(k0, s0, tile[:, :384])(0)
        put(k1, s1, tile[:, 384:])(0)

    @pl.when(step == 1)
    def _():
        tile = (dot(a_t[...], d_ref[0]) + dot(ar_t[...], dr_ref[0])).astype(bf16)
        put(k2, s2, tile[:, :384])(0)
        put(k0, s0, tile[:, 384:])(1)

    @pl.when(step == 2)
    def _():
        tile = (dot(a_t[...], d_ref[0]) + dot(ar_t[...], dr_ref[0])).astype(bf16)
        put(k1, s1, tile[:, :384])(1)
        put(k2, s2, tile[:, 384:])(1)


def late_call(me, a, ar, d, dr, after):
    def kern(*refs):
        return late_kernel(*refs[:5], *refs[5 + len(after) :])

    whole = pl.BlockSpec((SP, W), lambda i, *_: (0, 0))
    part = pl.BlockSpec((16, RB, 384), lambda i, *_: (0, 0, 0))
    res = pl.pallas_call(
        kern,
        grid_spec=pltpu.PrefetchScalarGridSpec(
            num_scalar_prefetch=1,
            grid=(3,),
            in_specs=[
                whole,
                whole,
                pl.BlockSpec((1, SP, W), lambda i, *_: (i, 0, 0)),
                pl.BlockSpec((1, SP, W), lambda i, *_: (jnp.maximum(i - 1, 0), 0, 0)),
            ] + [pl.BlockSpec(memory_space=pl.ANY)] * len(after),
            out_specs=[part] * 6,
            scratch_shapes=[pltpu.VMEM((W, SP), bf16)] * 2,
        ),
        out_shape=[S((16, RB, 384), bf16)] * 6,
        compiler_params=pltpu.CompilerParams(vmem_limit_bytes=56 * 1024 * 1024),
        cost_estimate=pl.CostEstimate(flops=6 * 10**9, bytes_accessed=14 * 10**6, transcendentals=0),
        name="late_grads",
    )(me, a, ar, d, dr, *after)
    return res[:3], res[3:]


def qkv_call(x, w_qkv, bias, vec, n, after, name):
    def kern(x_ref, w_ref, bias_ref, vec_ref, *refs):
        a_ref, out_ref = refs[len(after) :]
        a = (norm_one(x_ref)[0] * vec_ref[0:1] + vec_ref[1:2]).astype(bf16)
        a_ref[...] = a
        out_ref[...] = (dot(a, w_ref[:, (3 - n) * W :]) + bias_ref[0:1, (3 - n) * W :]).astype(bf16)

    rows = lambda width: pl.BlockSpec((MR, width), lambda i: (i, 0))
    return pl.pallas_call(
        kern,
        grid=(SP // MR,),
        in_specs=[
            rows(W),
            pl.BlockSpec((W, 3 * W), lambda i: (0, 0)),
            pl.BlockSpec((1, 3 * W), lambda i: (0, 0)),
            pl.BlockSpec((2, W), lambda i: (0, 0)),
        ] + [pl.BlockSpec(memory_space=pl.ANY)] * len(after),
        out_specs=[rows(W), rows(n * W)],
        out_shape=[S((SP, W), bf16), S((SP, n * W), bf16)],
        compiler_params=pltpu.CompilerParams(vmem_limit_bytes=56 * 1024 * 1024),
        cost_estimate=pl.CostEstimate(flops=n * 12 * 10**8, bytes_accessed=10**7, transcendentals=0),
        name=name,
    )(x, w_qkv, bias, vec, *after)


def norm_one(x_ref):
    x = x_ref[...].astype(f32)
    centered = x - rowmean(x)
    inv = lax.rsqrt(rowmean(centered * centered) + EPS)
    return centered * inv, inv


def input_kernel(x_ref, d_ref, w_ref, gain_ref, *refs):
    n = d_ref.shape[0]
    sums_ref = refs[-1]

    @pl.when(pl.program_id(0) == 0)
    def _():
        sums_ref[...] = jnp.zeros_like(sums_ref)

    x_hat, inv = norm_one(x_ref)
    part = None
    for i in range(n):
        a = tdot(d_ref[i], w_ref[:, (3 - n + i) * W : (4 - n + i) * W])
        part = a if part is None else part + a
    total = lambda a: jnp.sum(a.astype(f32), 0, keepdims=True)
    first = total(d_ref[0]) if n == 3 else jnp.zeros((1, W), f32)
    sums_ref[...] += jnp.concatenate(
        [first, total(d_ref[n - 1]), total(part * x_hat), total(part), jnp.zeros((4, W), f32)], 0
    )
    if n == 2:
        refs[0][...] = part.astype(bf16)
    else:
        returned_ref, gatt_ref = refs[:2]
        scaled = (part + returned_ref[0].astype(f32)) * gain_ref[0:1]
        inner = scaled - rowmean(scaled) - x_hat * rowmean(scaled * x_hat)
        refs[-2][...] = (gatt_ref[...].astype(f32) + inv * inner).astype(bf16)


def input_call(side, x, d, w_qkv, gain, extra, after, name):
    n = d.shape[0]
    rows = pl.BlockSpec((MR, W), lambda i, *_: (i, 0))
    more = [pl.BlockSpec((1, MR, W), lambda i, side_ref: (side_ref[0], i, 0)), rows] if extra else []
    skip = 5 + len(extra)

    def kern(*refs):
        return input_kernel(*refs[1:skip], *refs[skip + len(after) :])

    return pl.pallas_call(
        kern,
        grid_spec=pltpu.PrefetchScalarGridSpec(
            num_scalar_prefetch=1,
            grid=(SP // MR,),
            in_specs=[
                rows,
                pl.BlockSpec((n, MR, W), lambda i, *_: (0, i, 0)),
                pl.BlockSpec((W, 3 * W), lambda i, *_: (0, 0)),
                pl.BlockSpec((1, W), lambda i, *_: (0, 0)),
            ] + more + [pl.BlockSpec(memory_space=pl.ANY)] * len(after),
            out_specs=[rows, pl.BlockSpec((8, W), lambda i, *_: (0, 0))],
        ),
        out_shape=[S((SP, W), bf16), S((8, W), f32)],
        compiler_params=pltpu.CompilerParams(vmem_limit_bytes=56 * 1024 * 1024),
        cost_estimate=pl.CostEstimate(flops=n * 12 * 10**8, bytes_accessed=10**7, transcendentals=0),
        name=name,
    )(side, x, d, w_qkv, gain, *extra, *after)


def swap_spans(x):
    return lax.ppermute(x, "blk", [(0, 1), (1, 0)])


def rows_dot(left, right):
    return lax.dot_general(left, right, (((0,), (0,)), ((), ())), preferred_element_type=f32)


def body(
    inputs, cotangent, lengths, groups, flip,
    w_qkv, b_query, b_value, w_out, b_out, gain_one, shift_one, gain_two, shift_two,
    w_fc, b_fc, w_proj, b_proj,
):
    place = jnp.bitwise_xor(lax.axis_index("blk"), flip[0])
    klen = jnp.minimum(lengths[0] - place * SP, SP)
    place_s = place.reshape(1).astype(jnp.int32)
    klen_s = klen.reshape(1).astype(jnp.int32)
    x_b = inputs[0, 0]
    up_b = cotangent[0, 0]
    xr_b = swap_spans(x_b)

    qkv_bias = jnp.concatenate([b_query, jnp.zeros_like(b_value), b_value])[None]
    vec_one = jnp.stack([gain_one, shift_one])
    normed, qkv = qkv_call(x_b, w_qkv, qkv_bias, vec_one, 3, (), "own_qkv")
    c = col(0)
    tall = pl.BlockSpec((1, 128, SP), lambda j, *_: (j, 0, 0))
    od, ld = call(
        diag_fwd, place_s, klen_s, (qkv, qkv, qkv), [c, col(6), col(12)],
        [S((NP, 128, SP), f32), S((NP, 8, SP), f32)], [tall, ROW],
    )

    normed_r, kvr = qkv_call(xr_b, w_qkv, qkv_bias, vec_one, 2, (ld,), "other_kv")
    attended, lse = call(
        cross_fwd, place_s, klen_s, (qkv, kvr, kvr, od, ld), [c, c, col(6), tall, ROW],
        [S((SP, W), bf16), S((NP, 8, SP), f32)], [c, ROW],
    )

    zero = jnp.zeros_like(b_out)
    vec = jnp.stack([b_out, gain_two, shift_two, b_proj, zero, zero, zero, zero])
    outputs, activ, grad_pre, normed_two, grad_att, grad_attended, sums, grad_b_fc = block_call(
        klen_s, x_b, attended, up_b, w_out, w_fc, w_proj, vec, b_fc[None]
    )
    me = my_id()
    keeps, sends = grads_call(me, normed_two, grad_pre, activ, up_b, attended, grad_att)
    acc = pltpu.VMEM((128, SP), f32)
    flops = 8 * 10**9
    dqx = dkvr = delta = dqkv = None

    def cross_piece(at, pairs, dep):
        nonlocal dqx, dkvr, delta
        dqx, dkvr, delta = call(
            cross_bwd, place_s, klen_s, (qkv, kvr, kvr, grad_attended, attended, lse),
            [col(at), col(at), col(6 + at), col(at), col(at), row(at)],
            [S((SP, W), f32), S((2, SP, W), bf16), S((NP, 8, SP), f32)],
            [col(at), cols(2, at), row(at)], [acc], pairs=pairs,
            into={0: dqx, 1: dkvr, 2: delta} if at else None, after=dep, flops=flops * pairs,
        )

    def diag_piece(at, pairs, dep):
        nonlocal dqkv
        (dqkv,) = call(
            diag_bwd, place_s, klen_s, (qkv, qkv, qkv, grad_attended, lse, delta, dqx),
            [col(at), col(6 + at), col(12 + at), col(at), row(at), row(at), col(at)],
            [S((3, SP, W), bf16)], [cols(3, at)], [acc], pairs=pairs,
            into={0: dqkv} if at else None, after=dep, flops=flops * pairs // 2,
        )

    arrays = lambda state: [a for a, _ in state]
    gain = gain_one[None]
    side = (1 - lax.axis_index("blk")).astype(jnp.int32).reshape(1)
    cross_piece(0, 1, keeps)
    state = core_step(keeps, sends)
    cross_piece(1, 3, arrays(state))
    state = low_step(state, 0)
    cross_piece(4, 2, arrays(state))
    state = low_step(state, 1)
    part_r, sums_r = input_call(side, xr_b, dkvr, w_qkv, gain, (), arrays(state), "other_span")
    returned = lax.all_gather(part_r, "blk", axis=0, tiled=False)
    state = low_step(state, 2)
    diag_piece(0, 3, arrays(state) + [part_r])
    early_sum = last_step(state, [dqkv])
    diag_piece(3, 3, [early_sum])
    early = unpack_early(gather_all(early_sum))

    state = core_step(*late_call(me, normed, normed_r, dqkv, dkvr, []))
    input_grad, sums_o = input_call(
        side, x_b, dqkv, w_qkv, gain, (returned, grad_att), arrays(state), "input_grad"
    )
    state = low_step(state, 0, [sums_o])
    for step in (1, 2, 3):
        state = low_step(state, step)
    late = unpack_late(me, *spread_parts(outer_sum(arrays(state))))

    member = (groups[0] == jnp.arange(2, dtype=jnp.int32)).astype(f32)
    squares = jnp.concatenate([jnp.sum(sums[4:7], 1), klen.astype(f32)[None]])
    sums_one = sums_o + sums_r
    small = jnp.concatenate([
        sums_one[0], sums_one[1], sums[2], sums_one[2], sums_one[3], sums[0], sums[1], grad_b_fc[0], sums[3],
        (member[:, None] * squares[None, :]).reshape(-1), jnp.zeros((1016,), f32),
    ])
    small = sum_small(small.reshape(80, 128)).reshape(-1)
    sizes = [W] * 7 + [4 * W, W]
    pieces = []
    at = 0
    for size in sizes:
        pieces.append(small[at : at + size])
        at += size
    table = small[at : at + 8].reshape(2, 4)
    group_rms = jnp.sqrt(table[:, :3] / (table[:, 3:] * W))
    g_bq, g_bv, g_bo, g_g1, g_s1, g_g2, g_s2, g_bfc, g_bp = pieces
    return (
        outputs[None, None], input_grad[None, None], late, g_bq, g_bv, early[2], g_bo, g_g1, g_s1, g_g2, g_s2,
        early[0], g_bfc, early[1].reshape(4 * W, W), g_bp, group_rms,
    )


def solution(mesh):
    span = P("dp", "blk", None, None)
    return jax.shard_map(
        body,
        mesh=mesh,
        in_specs=(span, span, P("dp"), P("dp"), P("dp")) + (P(),) * 13,
        out_specs=(span, span) + (P(),) * 14,
        check_vma=False,
    )
```

time: 634 us -> 392 us (0.62)
  waiting for transfers between devices: 297 us -> 51.8 us
  Pallas kernels: 53.3 us -> 183 us
  matrix products: 114 us -> 0 us
  blocking collectives: 39.9 us -> 0 us
  starting transfers between devices: 50.4 us -> 89.8 us
  other arithmetic: 37.5 us -> 15 us
  local copies, waits for them, and re-layouts: 15 us -> 28.1 us
    psum x2 -> x0, waiting for transfers between devices: 258 us -> none  [the longest x1 219 us: body(): early = lax.psum((grad_w_proj, grad_w_fc, grad_w_out), ('blk', 'dp'))]
    pallas_call x4 -> x18, Pallas kernels: 53.3 us -> 183 us  [the longest x7 58.5 us: call(): pl.pallas_call(kern, grid_spec=pltpu.PrefetchScalarGridSpec(num_scalar_pr...]
    dot_general x21 -> x0, matrix products: 114 us -> none  [the longest x5 41.3 us: dot(): return jnp.dot(a, b, preferred_element_type=f32)]
    ppermute x0 -> x50, starting transfers between devices: none -> 86.8 us  [swap(): lax.ppermute(a, axis, [(i, i ^ step) for i in range(lax.axis_size(axis))])]
    ppermute x0 -> x50, waiting for transfers between devices: none -> 50.3 us  [swap(): lax.ppermute(a, axis, [(i, i ^ step) for i in range(lax.axis_size(axis))])]
    ppermute x2 -> x1, starting transfers between devices: 50 us -> 3 us  [swap_spans(): return lax.ppermute(x, 'blk', [(0, 1), (1, 0)])]
    psum x1 -> x0, blocking collectives: 39.9 us -> none  [body(): lax.psum(jnp.concatenate([grad_b_query, grad_b_value, jnp.sum(grad_att.as...]
    ppermute x2 -> x1, waiting for transfers between devices: 39.5 us -> 1.38 us  [swap_spans(): return lax.ppermute(x, 'blk', [(0, 1), (1, 0)])]
  transfers between devices with their start and end apart: 4 -> 53, of which waited for: 4 -> 19; matrix products, arithmetic and copies ran while one was open for 7% -> 9% of each run, Pallas kernels for 2% -> 26%
where the time goes in v2:
time: 392 us; the launch traced here: 385 us
  Pallas kernels  183 us (47%)
  starting transfers between devices  89.8 us (23%)
  waiting for transfers between devices  51.8 us (13%)
  local copies, waits for them, and re-layouts  28.1 us (7%)
  between operations  17.4 us (4%)
  other arithmetic  15 us (4%)
    ppermute x50, starting transfers between devices, swap(): lax.ppermute(a, axis, [(i, i ^ step) for i in range(lax.axis_size(axis))])  86.8 us
    pallas_call x7, Pallas kernels, call(): pl.pallas_call(kern, grid_spec=pltpu.PrefetchScalarGridSpec(num_scalar_pr...  58.5 us
    ppermute x50, waiting for transfers between devices, swap(): lax.ppermute(a, axis, [(i, i ^ step) for i in range(lax.axis_size(axis))])  50.3 us
    pallas_call x1, Pallas kernels, block_call(): pl.pallas_call(block_kernel, grid_spec=pltpu.PrefetchScalarGridSpec(num_s...  34.2 us
    pallas_call x1, Pallas kernels, grads_call(): pl.pallas_call(grads_kernel, grid_spec=pltpu.PrefetchScalarGridSpec(num_s...  23.1 us
    pallas_call x2, Pallas kernels, input_call(): pl.pallas_call(kern, grid_spec=pltpu.PrefetchScalarGridSpec(num_scalar_pr...  17.2 us
    pallas_call x2, Pallas kernels, qkv_call(): pl.pallas_call(kern, grid=(SP // MR,), in_specs=[rows(W), pl.BlockSpec((W...  15.9 us
    pallas_call x1, Pallas kernels, unpack_early(): pl.pallas_call(kern, grid=(16 // rows,), in_specs=[pl.BlockSpec(block, la...  12.1 us
  transfers between devices with their start and end apart: 53, of which 19 were waited for; matrix products, arithmetic and copies ran while one was open for 9% of the time, Pallas kernels for 26%

profile of v2, /device:TPU:0, one launch (start us, length us, event | category | flops | bytes accessed | tf_op | source)
XLA Modules:
  0.0 384.9 jit_solution(1447478655228831325)
XLA Ops:
  7.2 3.0 collective-permute-start
  17.6 8.4 %own_qkv.1 = (bf16[1024,768]{1,0:T(8,128)(2,1)}, bf16[1024,2304]{1,0:T(8,128)(2,1)}) custom-call(bf16[1024,768]{1,0:T(8,128)(2,1)} %bitcast.228, bf16[768,2304]{1,0:T(8,128)(2,1)} %refs_3_.3, f32[1,2304]{1,0:T(1,128)} %broadcast_in_dim.34.bias_ref, f32[2,768]{1,0:T(2,128)} %pad_maximum_fusion.11.vec_ref), custom_call_target="tpu_custom_call" | custom-call | flops 3600000000 | bytes 10000000 | tf_op jit(solution)/shard_map/own_qkv/pallas_call | solution.py:616
  26.0 14.4 %diag_fwd.1 = (f32[6,128,1024]{2,1,0:T(8,128)S(1)}, f32[6,8,1024]{2,1,0:T(8,128)S(1)}) custom-call(s32[1]{0:T(128)} %bitcast.4.refs_0_, s32[1]{0:T(128)} %bitcast.2.refs_1_.klen_ref, bf16[1024,2304]{1,0:T(8,128)(2,1)} %get-tuple-element.66.refs_2_.refs_3_.refs_4_, bf16[1024,2304]{1,0:T(8,128)(2,1)} %get-tuple-element.66.refs_2_.refs_3_.refs_4_, ...), custom_call_target="tpu_custom_call" | custom-call | bytes 60000 | tf_op jit(solution)/shard_map/diag_fwd/pallas_call | solution.py:154
  46.0 7.5 %other_kv.1 = (bf16[1024,768]{1,0:T(8,128)(2,1)}, bf16[1024,1536]{1,0:T(8,128)(2,1)}) custom-call(bf16[1024,768]{1,0:T(8,128)(2,1)} %copy-done.24, bf16[768,2304]{1,0:T(8,128)(2,1)} %refs_3_.3, f32[1,2304]{1,0:T(1,128)} %broadcast_in_dim.34.bias_ref, f32[2,768]{1,0:T(2,128)} %pad_maximum_fusion.11.vec_ref, f32[6,8,1024]{2,1,0:T(8,128)} %copy-done.2), custom_call_target="tpu_custom_call" | custom-call | flops 2400000000 | bytes 10000000 | tf_op jit(solution)/shard_map/other_kv/pallas_call | solution.py:616
  53.5 5.2 %cross_fwd.1 = (bf16[1024,768]{1,0:T(8,128)(2,1)S(1)}, f32[6,8,1024]{2,1,0:T(8,128)S(1)}) custom-call(s32[1]{0:T(128)} %bitcast.4.refs_0_, s32[1]{0:T(128)} %bitcast.2.refs_1_.klen_ref, bf16[1024,2304]{1,0:T(8,128)(2,1)} %get-tuple-element.66.refs_2_.refs_3_.refs_4_, bf16[1024,1536]{1,0:T(8,128)(2,1)} %get-tuple-element.68.refs_3_.refs_4_, ...), custom_call_target="tpu_custom_call" | custom-call | bytes 60000 | tf_op jit(solution)/shard_map/cross_fwd/pallas_call | solution.py:154
  59.9 34.2 %block_mlp.1 = (bf16[1024,768]{1,0:T(8,128)(2,1)}, bf16[1024,3072]{1,0:T(8,128)(2,1)}, bf16[1024,3072]{1,0:T(8,128)(2,1)}, bf16[1024,768]{1,0:T(8,128)(2,1)}, bf...) custom-call(s32[1]{0:T(128)} %bitcast.2.refs_1_.klen_ref, ...), custom_call_target="tpu_custom_call" | custom-call | flops 22000001024 | bytes 35000000 | tf_op jit(solution)/shard_map/block_mlp/pallas_call | solution.py:436
  94.2 23.1 %block_grads.1 = (bf16[16,48,1152]{2,1,0:T(8,128)(2,1)}, bf16[16,48,1152]{2,1,0:T(8,128)(2,1)}, bf16[16,48,1152]{2,1,0:T(8,128)(2,1)}, bf16[16,48,1152]{2,1,0:T(...) custom-call(s32[1]{0:T(128)} %bitcast.9.me_ref.refs_0_, ...), custom_call_target="tpu_custom_call" | custom-call | flops 11000000512 | bytes 30000000 | tf_op jit(solution)/shard_map/block_grads/pallas_call | solution.py:521
  117.2 13.9 %collective-permute-start.1 = (bf16[16,48,1152]{2,1,0:T(8,128)(2,1)}, bf16[16,48,1152]{2,1,0:T(8,128)(2,1)}, u32[]{:S(2)}, u32[]{:S(2)}) collective-permute-start(bf16[16,48,1152]{2,1,0:T(8,128)(2,1)} %get-tuple-element.84), channel_id=1, source_target_pairs={{0,2},{2,0},{4,6},{6,4},{8,10},{10,8},{12,14},{14,12},{16,18},{18,... | collective-permute-start | bytes 5308424 | tf_op jit(solution)/shard_map/ppermute | solution.py:172
  131.7 3.0 cross_bwd.3
  140.1 6.1 %collective-permute-start.4 = (bf16[2,2,2,48,1152]{4,3,2,1,0:T(8,128)(2,1)}, bf16[2,2,2,48,1152]{4,3,2,1,0:T(8,128)(2,1)}, u32[]{:S(2)}, u32[]{:S(2)}) collective-permute-start(bf16[2,2,2,48,1152]{4,3,2,1,0:T(8,128)(2,1)} %bitcast.14), channel_id=1, source_target_pairs={{0,1},{1,0},{2,3},{3,2},{4,5},{5,4},{6,7},{7,6},{8,9},{9,8},{10,11... | collective-permute-start | bytes 2654216 | tf_op jit(solution)/shard_map/ppermute | solution.py:172
  151.6 4.6 %cross_bwd.4 = (f32[1024,768]{1,0:T(8,128)}, bf16[2,1024,768]{2,1,0:T(8,128)(2,1)}, f32[6,8,1024]{2,1,0:T(8,128)S(1)}) custom-call(s32[1]{0:T(128)} %bitcast.4.refs_0_, s32[1]{0:T(128)} %bitcast.2.refs_1_.klen_ref, bf16[1024,2304]{1,0:T(8,128)(2,1)} %get-tuple-element.66.refs_2_.refs_3_.refs_4_, ...), custom_call_target="tpu_custom_call", output_to_operand_aliasing={{0}: (8, {}), {1}: (9, {}), {2}: (10, {})} | custom-call | flops 24000000000 | bytes 30000 | tf_op jit(solution)/shard_map/cross_bwd/pallas_call | solution.py:154
  156.2 9.4 %collective-permute-done.4 = bf16[2,2,2,48,1152]{4,3,2,1,0:T(8,128)(2,1)} collective-permute-done((bf16[2,2,2,48,1152]{4,3,2,1,0:T(8,128)(2,1)}, bf16[2,2,2,48,1152]{4,3,2,1,0:T(8,128)(2,1)}, u32[]{:S(2)}, u32[]{:S(2)}) %collective-permute-start.4) | collective-permute-done | bytes 884768 | tf_op jit(solution)/shard_map/ppermute | solution.py:172
  168.8 5.5 %collective-permute-start.9 = (bf16[2,2,48,1152]{3,2,1,0:T(8,128)(2,1)S(1)}, bf16[2,2,48,1152]{3,2,1,0:T(8,128)(2,1)S(1)}, u32[]{:S(2)}, u32[]{:S(2)}) collective-permute-start(bf16[2,2,48,1152]{3,2,1,0:T(8,128)(2,1)S(1)} %slice_bitcast_fusion.4), channel_id=1, source_target_pairs={{0,8},{2,10},{4,12},{6,14},{8,0},{10,2},{12,4},{14,6},{16,24},{18,... | collective-permute-start | bytes 1327112 | tf_op jit(solution)/shard_map/ppermute | solution.py:172
  177.1 3.3 cross_bwd.5
  181.2 12.0 %collective-permute-start.8 = (bf16[2,48,1152]{2,1,0:T(8,128)(2,1)}, bf16[2,48,1152]{2,1,0:T(8,128)(2,1)}, u32[]{:S(2)}, u32[]{:S(2)}) collective-permute-start(bf16[2,48,1152]{2,1,0:T(8,128)(2,1)} %slice_bitcast_fusion.14), channel_id=1, source_target_pairs={{0,8},{2,10},{4,12},{6,14},{8,0},{10,2},{12,4},{14,6},{16,24},{18,... | collective-permute-start | bytes 663560 | tf_op jit(solution)/shard_map/ppermute | solution.py:172
  196.1 7.2 %other_span.1 = (bf16[1024,768]{1,0:T(8,128)(2,1)}, f32[8,768]{1,0:T(8,128)}) custom-call(s32[1]{0:T(128)} %bitcast.8.refs_0_, bf16[1024,768]{1,0:T(8,128)(2,1)} %copy-done.24, bf16[2,1024,768]{2,1,0:T(8,128)(2,1)} %get-tuple-element.92.refs_2_.refs_4_, bf16[768,2304]{1,0:T(8,128)(2,1)} %refs_3_.3, f32[1,768]{1,0:T(1,128)} %copy-done.40, ...), custom_call_target="tpu_custom_call" | custom-call | flops 2400000000 | bytes 10000000 | tf_op jit(solution)/shard_map/other_span/pallas_call | solution.py:676
  213.5 14.2 %diag_bwd.2.refs_6_.refs_9_ = bf16[3,1024,768]{2,1,0:T(8,128)(2,1)} custom-call(s32[1]{0:T(128)} %bitcast.4.refs_0_, s32[1]{0:T(128)} %bitcast.2.refs_1_.klen_ref, bf16[1024,2304]{1,0:T(8,128)(2,1)} %get-tuple-element.66.refs_2_.refs_3_.refs_4_, bf16[1024,2304]{1,0:T(8,128)(2,1)} %get-tuple-element.66.refs_2_.refs_3_.refs_4_, ...), custom_call_target="tpu_custom_call" | custom-call | flops 12000000000 | bytes 30000 | tf_op jit(solution)/shard_map/diag_bwd/pallas_call | solution.py:154
  233.8 13.9 %diag_bwd.3.refs_3_.refs_2_ = bf16[3,1024,768]{2,1,0:T(8,128)(2,1)} custom-call(s32[1]{0:T(128)} %bitcast.4.refs_0_, s32[1]{0:T(128)} %bitcast.2.refs_1_.klen_ref, bf16[1024,2304]{1,0:T(8,128)(2,1)} %get-tuple-element.66.refs_2_.refs_3_.refs_4_, bf16[1024,2304]{1,0:T(8,128)(2,1)} %get-tuple-element.66.refs_2_.refs_3_.refs_4_, ...), custom_call_target="tpu_custom_call", output_to_operand_aliasing={{}: (9, {})} | custom-call | flops 12000000000 | bytes 30000 | tf_op jit(solution)/shard_map/diag_bwd/pallas_call | solution.py:154
  247.7 12.1 %late_grads.1 = (bf16[16,48,384]{2,1,0:T(8,128)(2,1)}, bf16[16,48,384]{2,1,0:T(8,128)(2,1)}, bf16[16,48,384]{2,1,0:T(8,128)(2,1)}, bf16[16,48,384]{2,1,0:T(8,128...) custom-call(s32[1]{0:T(128)} %bitcast.9.me_ref.refs_0_, bf16[1024,768]{1,0:T(8,128)(2,1)} %get-tuple-element.97.refs_1_, ...), custom_call_target="tpu_custom_call" | custom-call | flops 6000000000 | bytes 14000000 | tf_op jit(solution)/shard_map/late_grads/pallas_call | solution.py:586
  269.7 10.0 %input_grad.1 = (bf16[1024,768]{1,0:T(8,128)(2,1)}, f32[8,768]{1,0:T(8,128)}) custom-call(s32[1]{0:T(128)} %bitcast.8.refs_0_, bf16[1024,768]{1,0:T(8,128)(2,1)} %bitcast.230, bf16[3,1024,768]{2,1,0:T(8,128)(2,1)} %diag_bwd.3.refs_3_.refs_2_, bf16[768,2304]{1,0:T(8,128)(2,1)} %refs_3_.3, f32[1,768]{1,0:T(1,128)} %copy-done.40, ...), custom_call_target="tpu_custom_call" | custom-call | flops 3600000000 | bytes 10000000 | tf_op jit(solution)/shard_map/input_grad/pallas_call | solution.py:676
  299.2 3.0 collective-permute-start.23
  306.1 3.0 collective-permute-start.24
  309.2 8.9 %collective-permute-done.24 = bf16[48,384]{1,0:T(8,128)(2,1)S(1)} collective-permute-done((bf16[48,384]{1,0:T(8,128)(2,1)S(1)}, bf16[48,384]{1,0:T(8,128)(2,1)S(1)}, u32[]{:S(2)}, u32[]{:S(2)}) %collective-permute-start.24) | collective-permute-done | bytes 36896 | tf_op jit(solution)/shard_map/ppermute | solution.py:172
  318.3 2.8 collective-permute-done.38
  321.3 2.9 collective-permute-start.32
  332.0 2.9 collective-permute-done.26
  335.1 3.4 collective-permute-start.41
  340.2 3.2 collective-permute-start.28
  343.5 4.9 %collective-permute-done.34 = bf16[4,48,384]{2,1,0:T(8,128)(2,1)S(1)} collective-permute-done((bf16[4,48,384]{2,1,0:T(8,128)(2,1)S(1)}, bf16[4,48,384]{2,1,0:T(8,128)(2,1)S(1)}, u32[]{:S(2)}, u32[]{:S(2)}) %collective-permute-start.34) | collective-permute-done | bytes 147488 | tf_op jit(solution)/shard_map/ppermute | solution.py:172
  349.9 5.4 %collective-permute-done.35 = bf16[8,48,384]{2,1,0:T(8,128)(2,1)S(1)} collective-permute-done((bf16[8,48,384]{2,1,0:T(8,128)(2,1)S(1)}, bf16[8,48,384]{2,1,0:T(8,128)(2,1)S(1)}, u32[]{:S(2)}, u32[]{:S(2)}) %collective-permute-start.35) | collective-permute-done | bytes 294944 | tf_op jit(solution)/shard_map/ppermute | solution.py:172
  360.0 5.4 %unpack_late.1 = f32[768,2304]{1,0:T(8,128)} custom-call(s32[1]{0:T(128)} %bitcast.9.me_ref.refs_0_, bf16[16,48,384]{2,1,0:T(8,128)(2,1)} %copy-done.25, bf16[16,48,384]{2,1,0:T(8,128)(2,1)} %copy-done.27, bf16[16,48,384]{2,1,0:T(8,128)(2,1)} %copy-done.26, bf16[16,48,384]{2,1,0:T(8,128)(2,1)} %copy-done.32, bf16[16,48,384]{2,1,0:T(8,128)(2,1)} %copy-done.30, ...), custom_call_target="tpu_custom_call" | custom-call | bytes 10000000 | tf_op jit(solution)/shard_map/unpack_late/pallas_call | solution.py:345
  365.4 12.1 %unpack_early.1 = (f32[768,3072]{1,0:T(8,128)}, f32[2,1536,768]{2,1,0:T(8,128)}, f32[768,768]{1,0:T(8,128)}) custom-call(bf16[32,3,48,1152]{3,2,1,0:T(8,128)(2,1)} %bitcast.210, bf16[32,3,48,1152]{3,2,1,0:T(8,128)(2,1)} %bitcast.211, bf16[32,3,48,1152]{3,2,1,0:T(8,128)(2,1)} %bitcast.212, bf16[32,3,48,1152]{3,2,1,0:T(8,128)(2,1)} %bitcast.213), custom_call_target="tpu_custom_call" | custom-call | bytes 31850496 | tf_op jit(solution)/shard_map/unpack_early/pallas_call | solution.py:299
  (285 shorter events, 98.6 us)
Async XLA Ops:
  7.2 262.5 %all-gather.5.cloned.1.call-start = ((), (), s32[]{:S(2)}) async-start(), calls=%async_computation | async-start | bytes 4718592 | tf_op jit(solution)/shard_map/all_gather | solution.py:773
  7.2 37.6 %collective-permute-start = (bf16[1024,768]{1,0:T(8,128)(2,1)}, bf16[1024,768]{1,0:T(8,128)(2,1)S(1)}, u32[]{:S(2)}, u32[]{:S(2)}) collective-permute-start(bf16[1024,768]{1,0:T(8,128)(2,1)} %bitcast.227), channel_id=1, source_target_pairs={{0,1},{1,0},{2,3},{3,2},{4,5},{5,4},{6,7},{7,6},{8,9},{9,8},{10,11... | collective-permute-start | bytes 4718600 | tf_op jit(solution)/shard_map/ppermute | solution.py:697
  117.2 19.4 %collective-permute-start.1 = (bf16[16,48,1152]{2,1,0:T(8,128)(2,1)}, bf16[16,48,1152]{2,1,0:T(8,128)(2,1)}, u32[]{:S(2)}, u32[]{:S(2)}) collective-permute-start(bf16[16,48,1152]{2,1,0:T(8,128)(2,1)} %get-tuple-element.84), channel_id=1, source_target_pairs={{0,2},{2,0},{4,6},{6,4},{8,10},{10,8},{12,14},{14,12},{16,18},{18,... | collective-permute-start | bytes 5308424 | tf_op jit(solution)/shard_map/ppermute | solution.py:172
  131.2 14.9 %collective-permute-start.2 = (bf16[16,48,1152]{2,1,0:T(8,128)(2,1)}, bf16[16,48,1152]{2,1,0:T(8,128)(2,1)S(1)}, u32[]{:S(2)}, u32[]{:S(2)}) collective-permute-start(bf16[16,48,1152]{2,1,0:T(8,128)(2,1)} %get-tuple-element.85), channel_id=1, source_target_pairs={{0,2},{2,0},{4,6},{6,4},{8,10},{10,8},{12,14},{14,12},{16,18},{18,... | collective-permute-start | bytes 5308424 | tf_op jit(solution)/shard_map/ppermute | solution.py:172
  131.2 18.2 %collective-permute-start.3 = (bf16[16,48,1152]{2,1,0:T(8,128)(2,1)}, bf16[16,48,1152]{2,1,0:T(8,128)(2,1)S(1)}, u32[]{:S(2)}, u32[]{:S(2)}) collective-permute-start(bf16[16,48,1152]{2,1,0:T(8,128)(2,1)} %get-tuple-element.86), channel_id=1, source_target_pairs={{0,2},{2,0},{4,6},{6,4},{8,10},{10,8},{12,14},{14,12},{16,18},{18,... | collective-permute-start | bytes 5308424 | tf_op jit(solution)/shard_map/ppermute | solution.py:172
  140.1 25.5 %collective-permute-start.4 = (bf16[2,2,2,48,1152]{4,3,2,1,0:T(8,128)(2,1)}, bf16[2,2,2,48,1152]{4,3,2,1,0:T(8,128)(2,1)}, u32[]{:S(2)}, u32[]{:S(2)}) collective-permute-start(bf16[2,2,2,48,1152]{4,3,2,1,0:T(8,128)(2,1)} %bitcast.14), channel_id=1, source_target_pairs={{0,1},{1,0},{2,3},{3,2},{4,5},{5,4},{6,7},{7,6},{8,9},{9,8},{10,11... | collective-permute-start | bytes 2654216 | tf_op jit(solution)/shard_map/ppermute | solution.py:172
  147.8 20.6 %collective-permute-start.5 = (bf16[2,2,2,48,1152]{4,3,2,0,1:T(8,128)(2,1)S(1)}, bf16[2,2,2,48,1152]{4,3,2,0,1:T(8,128)(2,1)S(1)}, u32[]{:S(2)}, u32[]{:S(2)}) collective-permute-start(bf16[2,2,2,48,1152]{4,3,2,0,1:T(8,128)(2,1)S(1)} %bitcast.234), channel_id=1, source_target_pairs={{0,4},{2,6},{4,0},{6,2},{8,12},{10,14},{12,8},{14,10},{16,20},{18,... | collective-permute-start | bytes 2654216 | tf_op jit(solution)/shard_map/ppermute | solution.py:172
  150.0 24.4 %collective-permute-start.6 = (bf16[2,2,2,48,1152]{4,3,2,1,0:T(8,128)(2,1)S(1)}, bf16[2,2,2,48,1152]{4,3,2,1,0:T(8,128)(2,1)S(1)}, u32[]{:S(2)}, u32[]{:S(2)}) collective-permute-start(bf16[2,2,2,48,1152]{4,3,2,1,0:T(8,128)(2,1)S(1)} %slice_bitcast_fusion), channel_id=1, source_target_pairs={{0,8},{2,10},{4,12},{6,14},{8,0},{10,2},{12,4},{14,6},{16,24},{18,... | collective-permute-start | bytes 2654216 | tf_op jit(solution)/shard_map/ppermute | solution.py:172
  167.0 13.4 %collective-permute-start.7 = (bf16[2,2,48,1152]{3,2,1,0:T(8,128)(2,1)S(1)}, bf16[2,2,48,1152]{3,2,1,0:T(8,128)(2,1)S(1)}, u32[]{:S(2)}, u32[]{:S(2)}) collective-permute-start(bf16[2,2,48,1152]{3,2,1,0:T(8,128)(2,1)S(1)} %slice_bitcast_fusion.6), channel_id=1, source_target_pairs={{0,4},{2,6},{4,0},{6,2},{8,12},{10,14},{12,8},{14,10},{16,20},{18,... | collective-permute-start | bytes 1327112 | tf_op jit(solution)/shard_map/ppermute | solution.py:172
  168.8 24.4 %collective-permute-start.9 = (bf16[2,2,48,1152]{3,2,1,0:T(8,128)(2,1)S(1)}, bf16[2,2,48,1152]{3,2,1,0:T(8,128)(2,1)S(1)}, u32[]{:S(2)}, u32[]{:S(2)}) collective-permute-start(bf16[2,2,48,1152]{3,2,1,0:T(8,128)(2,1)S(1)} %slice_bitcast_fusion.4), channel_id=1, source_target_pairs={{0,8},{2,10},{4,12},{6,14},{8,0},{10,2},{12,4},{14,6},{16,24},{18,... | collective-permute-start | bytes 1327112 | tf_op jit(solution)/shard_map/ppermute | solution.py:172
  174.6 19.5 %collective-permute-start.11 = (bf16[2,2,48,1152]{3,2,1,0:T(8,128)(2,1)S(1)}, bf16[2,2,48,1152]{3,2,1,0:T(8,128)(2,1)S(1)}, u32[]{:S(2)}, u32[]{:S(2)}) collective-permute-start(bf16[2,2,48,1152]{3,2,1,0:T(8,128)(2,1)S(1)} %slice_bitcast_fusion.2), channel_id=1, source_target_pairs={{0,1},{1,0},{2,3},{3,2},{4,5},{5,4},{6,7},{7,6},{8,9},{9,8},{10,11... | collective-permute-start | bytes 1327112 | tf_op jit(solution)/shard_map/ppermute | solution.py:172
  181.2 22.2 %collective-permute-start.8 = (bf16[2,48,1152]{2,1,0:T(8,128)(2,1)}, bf16[2,48,1152]{2,1,0:T(8,128)(2,1)}, u32[]{:S(2)}, u32[]{:S(2)}) collective-permute-start(bf16[2,48,1152]{2,1,0:T(8,128)(2,1)} %slice_bitcast_fusion.14), channel_id=1, source_target_pairs={{0,8},{2,10},{4,12},{6,14},{8,0},{10,2},{12,4},{14,6},{16,24},{18,... | collective-permute-start | bytes 663560 | tf_op jit(solution)/shard_map/ppermute | solution.py:172
  194.1 13.1 %collective-permute-start.10 = (bf16[2,48,1152]{2,1,0:T(8,128)(2,1)}, bf16[2,48,1152]{2,1,0:T(8,128)(2,1)}, u32[]{:S(2)}, u32[]{:S(2)}) collective-permute-start(bf16[2,48,1152]{2,1,0:T(8,128)(2,1)} %slice_bitcast_fusion.12), channel_id=1, source_target_pairs={{0,1},{1,0},{2,3},{3,2},{4,5},{5,4},{6,7},{7,6},{8,9},{9,8},{10,11... | collective-permute-start | bytes 663560 | tf_op jit(solution)/shard_map/ppermute | solution.py:172
  194.3 15.6 %collective-permute-start.12 = (bf16[2,48,1152]{2,1,0:T(8,128)(2,1)S(1)}, bf16[2,48,1152]{2,1,0:T(8,128)(2,1)}, u32[]{:S(2)}, u32[]{:S(2)}) collective-permute-start(bf16[2,48,1152]{2,1,0:T(8,128)(2,1)S(1)} %slice_bitcast_fusion.10), channel_id=1, source_target_pairs={{0,4},{2,6},{4,0},{6,2},{8,12},{10,14},{12,8},{14,10},{16,20},{18,... | collective-permute-start | bytes 663560 | tf_op jit(solution)/shard_map/ppermute | solution.py:172
  203.4 162.0 %all-gather.7.cloned.1.call-start = ((), (), s32[]{:S(2)}) async-start(), calls=%async_computation.1 | async-start | bytes 10948608 | tf_op jit(solution)/shard_map/all_gather | solution.py:274
  205.2 22.5 %collective-permute-start.13 = (bf16[48,1152]{1,0:T(8,128)(2,1)S(1)}, bf16[48,1152]{1,0:T(8,128)(2,1)S(1)}, u32[]{:S(2)}, u32[]{:S(2)}) collective-permute-start(bf16[48,1152]{1,0:T(8,128)(2,1)S(1)} %get-tuple-element.148), channel_id=1, source_target_pairs={{0,16},{2,18},{4,20},{6,22},{8,24},{10,26},{12,28},{14,30},{16,0},... | collective-permute-start | bytes 331784 | tf_op jit(solution)/shard_map/ppermute | solution.py:172
  208.9 18.8 %collective-permute-start.14 = (bf16[48,1152]{1,0:T(8,128)(2,1)S(1)}, bf16[48,1152]{1,0:T(8,128)(2,1)S(1)}, u32[]{:S(2)}, u32[]{:S(2)}) collective-permute-start(bf16[48,1152]{1,0:T(8,128)(2,1)S(1)} %get-tuple-element.146), channel_id=1, source_target_pairs={{0,16},{2,18},{4,20},{6,22},{8,24},{10,26},{12,28},{14,30},{16,0},... | collective-permute-start | bytes 331784 | tf_op jit(solution)/shard_map/ppermute | solution.py:172
  211.5 16.2 %collective-permute-start.15 = (bf16[48,1152]{1,0:T(8,128)(2,1)S(1)}, bf16[48,1152]{1,0:T(8,128)(2,1)S(1)}, u32[]{:S(2)}, u32[]{:S(2)}) collective-permute-start(bf16[48,1152]{1,0:T(8,128)(2,1)S(1)} %get-tuple-element.144), channel_id=1, source_target_pairs={{0,16},{2,18},{4,20},{6,22},{8,24},{10,26},{12,28},{14,30},{16,0},... | collective-permute-start | bytes 331784 | tf_op jit(solution)/shard_map/ppermute | solution.py:172
  264.1 16.5 %collective-permute-start.19 = (bf16[2,2,2,48,384]{4,3,2,1,0:T(8,128)(2,1)S(1)}, bf16[2,2,2,48,384]{4,3,2,1,0:T(8,128)(2,1)S(1)}, u32[]{:S(2)}, u32[]{:S(2)}) collective-permute-start(bf16[2,2,2,48,384]{4,3,2,1,0:T(8,128)(2,1)S(1)} %bitcast.243), channel_id=1, source_target_pairs={{0,1},{1,0},{2,3},{3,2},{4,5},{5,4},{6,7},{7,6},{8,9},{9,8},{10,11... | collective-permute-start | bytes 884744 | tf_op jit(solution)/shard_map/ppermute | solution.py:172
  266.6 14.1 %collective-permute-start.20 = (bf16[2,2,2,48,384]{4,3,2,1,0:T(8,128)(2,1)S(1)}, bf16[2,2,2,48,384]{4,3,2,1,0:T(8,128)(2,1)S(1)}, u32[]{:S(2)}, u32[]{:S(2)}) collective-permute-start(bf16[2,2,2,48,384]{4,3,2,1,0:T(8,128)(2,1)S(1)} %get-tuple-element.136), channel_id=1, source_target_pairs={{0,4},{2,6},{4,0},{6,2},{8,12},{10,14},{12,8},{14,10},{16,20},{18,... | collective-permute-start | bytes 884744 | tf_op jit(solution)/shard_map/ppermute | solution.py:172
  268.3 12.4 %collective-permute-start.21 = (bf16[2,2,2,48,384]{4,3,2,1,0:T(8,128)(2,1)S(1)}, bf16[2,2,2,48,384]{4,3,2,1,0:T(8,128)(2,1)S(1)}, u32[]{:S(2)}, u32[]{:S(2)}) collective-permute-start(bf16[2,2,2,48,384]{4,3,2,1,0:T(8,128)(2,1)S(1)} %get-tuple-element.134), channel_id=1, source_target_pairs={{0,8},{2,10},{4,12},{6,14},{8,0},{10,2},{12,4},{14,6},{16,24},{18,... | collective-permute-start | bytes 884744 | tf_op jit(solution)/shard_map/ppermute | solution.py:172
  285.5 9.1 %collective-permute-start.29 = (bf16[2,2,48,384]{3,2,1,0:T(8,128)(2,1)S(1)}, bf16[2,2,48,384]{3,2,1,0:T(8,128)(2,1)S(1)}, u32[]{:S(2)}, u32[]{:S(2)}) collective-permute-start(bf16[2,2,48,384]{3,2,1,0:T(8,128)(2,1)S(1)} %slice_bitcast_fusion.16), channel_id=1, source_target_pairs={{0,8},{2,10},{4,12},{6,14},{8,0},{10,2},{12,4},{14,6},{16,24},{18,... | collective-permute-start | bytes 442376 | tf_op jit(solution)/shard_map/ppermute | solution.py:172
  294.7 11.2 %collective-permute-start.30 = (bf16[2,48,384]{2,1,0:T(8,128)(2,1)S(1)}, bf16[2,48,384]{2,1,0:T(8,128)(2,1)S(1)}, u32[]{:S(2)}, u32[]{:S(2)}) collective-permute-start(bf16[2,48,384]{2,1,0:T(8,128)(2,1)S(1)} %slice_bitcast_fusion.26), channel_id=1, source_target_pairs={{0,1},{1,0},{2,3},{3,2},{4,5},{5,4},{6,7},{7,6},{8,9},{9,8},{10,11... | collective-permute-start | bytes 221192 | tf_op jit(solution)/shard_map/ppermute | solution.py:172
  297.5 11.6 %collective-permute-start.37 = (bf16[2,48,384]{2,1,0:T(8,128)(2,1)S(1)}, bf16[2,48,384]{2,1,0:T(8,128)(2,1)S(1)}, u32[]{:S(2)}, u32[]{:S(2)}) collective-permute-start(bf16[2,48,384]{2,1,0:T(8,128)(2,1)S(1)} %slice_bitcast_fusion.24), channel_id=1, source_target_pairs={{0,4},{2,6},{4,0},{6,2},{8,12},{10,14},{12,8},{14,10},{16,20},{18,... | collective-permute-start | bytes 221192 | tf_op jit(solution)/shard_map/ppermute | solution.py:172
  306.0 15.3 %collective-permute-start.31 = (bf16[48,384]{1,0:T(8,128)(2,1)S(1)}, bf16[48,384]{1,0:T(8,128)(2,1)S(1)}, u32[]{:S(2)}, u32[]{:S(2)}) collective-permute-start(bf16[48,384]{1,0:T(8,128)(2,1)S(1)} %slice_bitcast_fusion.32), channel_id=1, source_target_pairs={{0,16},{2,18},{4,20},{6,22},{8,24},{10,26},{12,28},{14,30},{16,0},... | collective-permute-start | bytes 110600 | tf_op jit(solution)/shard_map/ppermute | solution.py:172
  306.1 12.0 %collective-permute-start.24 = (bf16[48,384]{1,0:T(8,128)(2,1)S(1)}, bf16[48,384]{1,0:T(8,128)(2,1)S(1)}, u32[]{:S(2)}, u32[]{:S(2)}) collective-permute-start(bf16[48,384]{1,0:T(8,128)(2,1)S(1)} %slice_bitcast_fusion.34), channel_id=1, source_target_pairs={{0,16},{2,18},{4,20},{6,22},{8,24},{10,26},{12,28},{14,30},{16,0},... | collective-permute-start | bytes 110600 | tf_op jit(solution)/shard_map/ppermute | solution.py:172
  309.1 12.0 %collective-permute-start.38 = (bf16[48,384]{1,0:T(8,128)(2,1)S(1)}, bf16[48,384]{1,0:T(8,128)(2,1)S(1)}, u32[]{:S(2)}, u32[]{:S(2)}) collective-permute-start(bf16[48,384]{1,0:T(8,128)(2,1)S(1)} %slice_bitcast_fusion.30), channel_id=1, source_target_pairs={{0,16},{2,18},{4,20},{6,22},{8,24},{10,26},{12,28},{14,30},{16,0},... | collective-permute-start | bytes 110600 | tf_op jit(solution)/shard_map/ppermute | solution.py:172
  321.3 9.3 %collective-permute-start.32 = (bf16[1,48,384]{2,1,0:T(8,128)(2,1)S(1)}, bf16[1,48,384]{2,1,0:T(8,128)(2,1)S(1)}, u32[]{:S(2)}, u32[]{:S(2)}) collective-permute-start(bf16[1,48,384]{2,1,0:T(8,128)(2,1)S(1)} %get-tuple-element.127), channel_id=1, source_target_pairs={{0,16},{2,18},{4,20},{6,22},{8,24},{10,26},{12,28},{14,30},{16,0},... | collective-permute-start | bytes 110600 | tf_op jit(solution)/shard_map/ppermute | solution.py:172
  325.8 9.1 %collective-permute-start.26 = (bf16[2,48,384]{2,1,0:T(8,128)(2,1)S(1)}, bf16[2,48,384]{2,1,0:T(8,128)(2,1)S(1)}, u32[]{:S(2)}, u32[]{:S(2)}) collective-permute-start(bf16[2,48,384]{2,1,0:T(8,128)(2,1)S(1)} %pad_maximum_fusion.7), channel_id=1, source_target_pairs={{0,8},{2,10},{4,12},{6,14},{8,0},{10,2},{12,4},{14,6},{16,24},{18,... | collective-permute-start | bytes 221192 | tf_op jit(solution)/shard_map/ppermute | solution.py:172
  338.5 10.0 %collective-permute-start.34 = (bf16[4,48,384]{2,1,0:T(8,128)(2,1)S(1)}, bf16[4,48,384]{2,1,0:T(8,128)(2,1)S(1)}, u32[]{:S(2)}, u32[]{:S(2)}) collective-permute-start(bf16[4,48,384]{2,1,0:T(8,128)(2,1)S(1)} %pad_maximum_fusion.5), channel_id=1, source_target_pairs={{0,8},{2,10},{4,12},{6,14},{8,0},{10,2},{12,4},{14,6},{16,24},{18,... | collective-permute-start | bytes 442376 | tf_op jit(solution)/shard_map/ppermute | solution.py:172
  340.2 15.9 %collective-permute-start.28 = (bf16[8,48,384]{2,1,0:T(8,128)(2,1)S(1)}, bf16[8,48,384]{2,1,0:T(8,128)(2,1)S(1)}, u32[]{:S(2)}, u32[]{:S(2)}) collective-permute-start(bf16[8,48,384]{2,1,0:T(8,128)(2,1)S(1)} %pad_maximum_fusion.1), channel_id=1, source_target_pairs={{0,1},{1,0},{2,3},{3,2},{4,5},{5,4},{6,7},{7,6},{8,9},{9,8},{10,11... | collective-permute-start | bytes 884744 | tf_op jit(solution)/shard_map/ppermute | solution.py:172
  343.4 12.0 %collective-permute-start.42 = (bf16[8,48,384]{2,1,0:T(8,128)(2,1)S(1)}, bf16[8,48,384]{2,1,0:T(8,128)(2,1)S(1)}, u32[]{:S(2)}, u32[]{:S(2)}) collective-permute-start(bf16[8,48,384]{2,1,0:T(8,128)(2,1)S(1)} %pad_maximum_fusion.3), channel_id=1, source_target_pairs={{0,8},{2,10},{4,12},{6,14},{8,0},{10,2},{12,4},{14,6},{16,24},{18,... | collective-permute-start | bytes 884744 | tf_op jit(solution)/shard_map/ppermute | solution.py:172
  (65 other events, 365.8 us)
Sparse Core Ops, SparseCore 0:
  203.5 44.4 all-gather.4
  250.9 98.2 all-gather.6
